TPU v7x, 128 devices: a whole 4x4x4 slice. The times are simulated.
128 devices in a mesh: row: 8 (over z, core), col: 16 (over y, x).
Axes of the slice: x: 4, y: 4, z: 4, core: 2. Of those that a mesh axis runs over, the one named last changes fastest.
Arguments:
- embeddings: bfloat16 [40960, 256], P(('row', 'col')), may hold values from -90 to 90
- start_vectors: float32 [32, 40960], P(None, ('row', 'col')), may hold values from -6 to 6
Outputs:
- vectors: float32 [32, 40960], P(None, ('row', 'col'))
- degrees: float32 [40960], P(('row', 'col'))
All inputs are finite; a program needn't handle non-finite values.
Results may differ from a plain program's by a relative error of at most 0.015.
Values may be sent and summed in bfloat16 or wider, within the bound.
A program may use at most 128 MiB of HBM per device.

v0:
```python
import math

import jax
import jax.numpy as jnp
from jax import lax
from jax.sharding import PartitionSpec as P

ITERS = 2


def normalize(embeddings):
    values = embeddings.astype(jnp.float32)
    power = jnp.mean(values * values, axis=1, keepdims=True)
    width = embeddings.shape[1]
    return (values * lax.rsqrt(power + 1e-06) / jnp.sqrt(jnp.float32(width))).astype(jnp.bfloat16)


def build_tile(row_emb, col_emb):
    total_rows = row_emb.shape[0]
    step_rows = math.gcd(total_rows, 512)
    pieces = row_emb.reshape(total_rows // step_rows, step_rows, row_emb.shape[1])

    def one_piece(piece):
        inner = lax.dot_general(
            piece, col_emb, (((1,), (1,)), ((), ())), preferred_element_type=jnp.float32
        )
        return jnp.exp(8.0 * (inner - 1.0)).astype(jnp.bfloat16)

    return lax.map(one_piece, pieces).reshape(total_rows, col_emb.shape[0])


def local(embeddings, start_vectors):
    own_unit = normalize(embeddings)
    row_emb = lax.all_gather(own_unit, "col", axis=0, tiled=True)
    col_emb = lax.all_gather(own_unit, "row", axis=0, tiled=True)
    tile = build_tile(row_emb, col_emb)
    partial_rows = jnp.sum(tile, axis=1, dtype=jnp.float32)
    degrees = lax.psum_scatter(partial_rows, "col", scatter_dimension=0, tiled=True)
    scale = 1.0 / jnp.sqrt(degrees)
    current = start_vectors
    for step in range(ITERS):
        scaled = (current * scale[None, :]).astype(jnp.bfloat16)
        partial_value = lax.dot_general(
            lax.all_gather(scaled, "row", axis=1, tiled=True),
            tile,
            (((1,), (1,)), ((), ())),
            preferred_element_type=jnp.float32,
        )
        summed = lax.psum_scatter(
            partial_value.astype(jnp.bfloat16), "col", scatter_dimension=1, tiled=True
        ).astype(jnp.float32)
        image = summed * scale[None, :]
        local_gram = jnp.dot(image, image.T, precision=lax.Precision.HIGHEST)
        gram = lax.psum(local_gram, ("row", "col"))
        lower = jnp.linalg.cholesky(gram)
        current = lax.linalg.triangular_solve(lower, image, left_side=True, lower=True)
    return (current, degrees)


def solution(mesh):
    return jax.shard_map(
        local,
        mesh=mesh,
        in_specs=(P(("row", "col"), None), P(None, ("row", "col"))),
        out_specs=(P(None, ("row", "col")), P(("row", "col"))),
        check_vma=False,
    )
```

profile of v0, /device:TPU:1, one launch (start us, length us, event | category | flops | bytes accessed | tf_op | source)
XLA Modules:
  0.0 554.1 jit_solution(16428623404612519531)
XLA Ops:
  7.2 1.1 fusion.7
  8.3 1.7 fusion.9
  10.8 1.2 dynamic-slice
  12.7 25.4 %all-gather.7.cloned.1.call-done = bf16[2560,256]{1,0:T(8,128)(2,1)} async-done(((bf16[320,256]{1,0:T(8,128)(2,1)}), bf16[2560,256]{1,0:T(8,128)(2,1)}) %all-gather.7.cloned.1.call-update) | async-done | bytes 1310736 | tf_op jit(solution)/shard_map/all_gather | solution.py:35
  38.1 47.5 %all-gather.5.cloned.1.call-done = bf16[5120,256]{1,0:T(8,128)(2,1)} async-done(((bf16[320,256]{1,0:T(8,128)(2,1)}), bf16[5120,256]{1,0:T(8,128)(2,1)}) %all-gather.5.cloned.1.call-update) | async-done | bytes 2621456 | tf_op jit(solution)/shard_map/all_gather | solution.py:34
  85.6 39.4 %while.12 = (s32[]{:T(128)}, bf16[10,512,2560]{2,1,0:T(8,128)(2,1)}, bf16[10,512,256]{2,1,0:T(8,128)(2,1)}, bf16[2560,256]{1,0:T(8,128)(2,1)}, s32[]{:T(128)}) while((s32[]{:T(128)}, bf16[10,512,2560]{2,1,0:T(8,128)(2,1)}, bf16[10,512,256]{2,1,0:T(8,128)(2,1)}, bf16[2560,256]{1,0:T(8,128)(2,1)}, s32[]{:T(128)}) %tuple.44), condition=%wide.region_2.3_spmd, body=%wide.region_1.2_spmd.sunk | while | flops 675020800 | bytes 4195389 | solution.py:29
  85.6 3.9 fusion.37
  89.5 4.0 fusion.37
  93.5 3.9 fusion.37
  97.4 4.0 fusion.37
  101.4 3.9 fusion.37
  105.4 3.9 fusion.37
  109.3 3.9 fusion.37
  113.2 3.9 fusion.37
  117.1 4.0 fusion.37
  121.0 4.0 fusion.37
  125.0 9.5 %convert_reduce_fusion = f32[10,512]{1,0:T(8,128)S(1)} fusion(bf16[10,512,2560]{2,1,0:T(8,128)(2,1)} %get-tuple-element.57), kind=kLoop, calls=%fused_computation.6 | loop fusion | flops 26209280 | bytes 26234880 | tf_op jit(solution)/shard_map/reduce_sum | solution.py:37
  134.5 58.2 %all-reduce = f32[5120]{0:T(1024)S(1)} all-reduce(f32[5120]{0:T(1024)S(1)} %reduce_sum.22), channel_id=2, replica_groups=mesh['row'=8,'col'=16] {'col'}, use_global_device_ids=true, to_apply=%region_4.5.clone | all-reduce | flops 5120 | bytes 40960
  193.3 28.1 %all-gather = bf16[8,320,32]{1,2,0:T(8,128)(2,1)S(1)} all-gather(bf16[1,320,32]{1,2,0:T(8,128)(2,1)S(1)} %fusion.13), channel_id=1, replica_groups=mesh['row'=8,'col'=16] {'row'}, dimensions={0}, use_global_device_ids=true | all-gather | bytes 184320 | tf_op jit(solution)/shard_map/all_gather | solution.py:44
  221.6 12.6 %convolution_convert_fusion.1 = bf16[32,5120]{1,0:T(8,128)(2,1)S(1)} fusion(bf16[2560,32]{0,1:T(8,128)(2,1)S(1)} %reshape.36, bf16[5120,2560]{1,0:T(8,128)(2,1)} %bitcast.55), kind=kOutput, calls=%fused_computation.8 | convolution fusion | flops 839024640 | bytes 26705920 | tf_op jit(solution)/shard_map/dot_general | solution.py:43
  234.3 1.4 copy.22
  235.7 66.9 %reduce-scatter.7.cloned.1.call-done = bf16[320,32]{1,0:T(8,128)(2,1)} async-done(((bf16[5120,32]{1,0:T(8,128)(2,1)}), bf16[320,32]{1,0:T(8,128)(2,1)}) %reduce-scatter.7.cloned.1.call-update) | async-done | bytes 20496
  303.8 66.2 %psum.14 = f32[32,32]{0,1:T(8,128)S(1)} all-reduce(f32[32,32]{0,1:T(8,128)S(1)} %fusion.12), channel_id=1, replica_groups=mesh['row'=8,'col'=16] {'row','col'}, use_global_device_ids=true, to_apply=%region_6.7 | all-reduce | flops 1024 | bytes 8192 | tf_op jit(solution)/shard_map/psum | solution.py:54
  370.0 2.9 cholesky.44
  374.3 2.4 custom-call.6
  377.0 13.7 %all-gather.1 = bf16[8,320,32]{1,2,0:T(8,128)(2,1)S(1)} all-gather(bf16[1,320,32]{1,2,0:T(8,128)(2,1)S(1)} %fusion.6), channel_id=1, replica_groups=mesh['row'=8,'col'=16] {'row'}, dimensions={0}, use_global_device_ids=true | all-gather | bytes 184320 | tf_op jit(solution)/shard_map/all_gather | solution.py:44
  390.9 12.6 %convolution_convert_fusion = bf16[32,5120]{1,0:T(8,128)(2,1)S(1)} fusion(bf16[2560,32]{0,1:T(8,128)(2,1)S(1)} %reshape.38, bf16[5120,2560]{1,0:T(8,128)(2,1)} %bitcast.56), kind=kOutput, calls=%fused_computation.7 | convolution fusion | flops 839024640 | bytes 26705920 | tf_op jit(solution)/shard_map/dot_general | solution.py:43
  403.6 1.4 copy.24
  405.0 67.6 %reduce-scatter.9.cloned.1.call-done = bf16[320,32]{1,0:T(8,128)(2,1)} async-done(((bf16[5120,32]{1,0:T(8,128)(2,1)}), bf16[320,32]{1,0:T(8,128)(2,1)}) %reduce-scatter.9.cloned.1.call-update) | async-done | bytes 20496
  473.8 66.1 %psum.15 = f32[32,32]{0,1:T(8,128)S(1)} all-reduce(f32[32,32]{0,1:T(8,128)S(1)} %fusion.11), channel_id=1, replica_groups=mesh['row'=8,'col'=16] {'row','col'}, use_global_device_ids=true, to_apply=%region_10.13 | all-reduce | flops 1024 | bytes 8192 | tf_op jit(solution)/shard_map/psum | solution.py:54
  540.0 2.9 cholesky.55
  544.3 2.4 custom-call.7
  (35 shorter events, 8.3 us)
Async XLA Ops:
  7.2 30.9 %all-gather.7.cloned.1.call-start = ((), (), s32[]{:S(2)}) async-start(), calls=%async_computation.3 | async-start | bytes 1474560 | tf_op jit(solution)/shard_map/all_gather | solution.py:35
  10.0 75.6 %all-gather.5.cloned.1.call-start = ((), (), s32[]{:S(2)}) async-start(), calls=%async_computation.2 | async-start | bytes 2785280 | tf_op jit(solution)/shard_map/all_gather | solution.py:34
  10.8 291.9 %reduce-scatter.7.cloned.1.call-start = ((), (), s32[]{:S(2)}) async-start(), calls=%async_computation.4 | async-start | bytes 1392640
  125.0 68.3 %copy-start = (f32[32,320]{1,0:T(8,128)S(1)}, f32[32,320]{1,0:T(8,128)}, u32[]{:S(2)}) copy-start(f32[32,320]{1,0:T(8,128)} %param.8) | copy-start | bytes 122884
  235.7 236.9 %reduce-scatter.9.cloned.1.call-start = ((), (), s32[]{:S(2)}) async-start(), calls=%async_computation.5 | async-start | bytes 1392640
Sparse Core Ops, SparseCore 0:
  10.1 27.9 all-gather.6
  40.2 45.3 all-gather.4
  235.8 66.7 reduce-scatter.6
  405.1 67.4 reduce-scatter.8
where the time goes:
time: 555 us; the launch traced here: 554 us
  blocking collectives  232 us (42%)
  waiting for transfers between devices  208 us (37%)
  matrix products  66.3 us (12%)
  other arithmetic  25.6 us (5%)
  between operations  14.5 us (3%)
  local copies, waits for them, and re-layouts  7.21 us (1%)
    unnamed x6, waiting for transfers between devices  135 us
    psum x2, blocking collectives, local(): gram = lax.psum(local_gram, ('row', 'col'))  132 us
    unnamed x1, blocking collectives  58.2 us
    all_gather x1, waiting for transfers between devices, local(): row_emb = lax.all_gather(own_unit, 'col', axis=0, tiled=True)  47.5 us
    all_gather x2, blocking collectives, local(): lax.all_gather(scaled, 'row', axis=1, tiled=True)  41.8 us
    dot_general x10, matrix products, one_piece(): lax.dot_general(piece, col_emb, (((1,), (1,)), ((), ())), preferred_eleme...  39.4 us
    all_gather x1, waiting for transfers between devices, local(): col_emb = lax.all_gather(own_unit, 'row', axis=0, tiled=True)  25.4 us
    dot_general x2, matrix products, local(): lax.dot_general(lax.all_gather(scaled, 'row', axis=1, tiled=True), tile,...  25.3 us
  transfers between devices with their start and end apart: 4, of which 4 were waited for; matrix products, arithmetic and copies ran while one was open for 0% of the time, Pallas kernels for 0%

commit v1 on v0

v1 whole, which is shorter than its diff:
```python
import functools
import math

import jax
import jax.numpy as jnp
from jax import lax
from jax.experimental import pallas as pl
from jax.experimental.pallas import tpu as pltpu
from jax.sharding import PartitionSpec as P

ITERS = 2
K = 32
E = 256
OWN = 320
NB = 128
NA = OWN - NB
NZ = 8
NQ = 4
J = NZ * OWN
RATE = 8.0 / math.log(2.0)
MESH = pl.DeviceIdType.MESH
HIGH = lax.Precision.HIGHEST
F32 = jnp.float32
BF16 = jnp.bfloat16


def dot_nt(a, b, precision=None):
    return lax.dot_general(a, b, (((1,), (1,)), ((), ())), precision=precision, preferred_element_type=F32)


def pack(square):
    return jnp.concatenate([square[8 * b : 8 * b + 8, :] for b in range(4)], axis=1)


def unpack(packed):
    return jnp.concatenate([packed[:, K * b : K * b + K] for b in range(4)], axis=0)


def inverse_factor(gram):
    rows = lax.broadcasted_iota(jnp.int32, (K, K), 0)
    columns = lax.broadcasted_iota(jnp.int32, (K, K), 1)
    eye = (rows == columns).astype(F32)
    work = jnp.concatenate([gram, eye], axis=1)
    below = lax.broadcasted_iota(jnp.int32, (K, 1), 0)
    pivots = jnp.ones((K, 1), F32)
    for k in range(K):
        pivot = work[k : k + 1, k : k + 1]
        column = work[:, k : k + 1]
        factor = jnp.where(below > k, column / pivot, 0.0)
        pivots = jnp.where(below == k, pivot, pivots)
        work = work - factor * work[k : k + 1, :]
    return work[:, K : 2 * K] * (1.0 / jnp.sqrt(pivots))


def kernel(
    emb_ref, start_ref, vec_ref, deg_ref,
    u_a, u_b, u_j, t_a, t_b, acc, start_all, part_send, part_recv, scale_all,
    lhs, send_a, send_b, recv_a, recv_b, raw_all, gram_z, gram_xy, image_ref,
    s_a, r_a, s_b, r_b, s_z, r_z, s_st, r_st, s_pt, r_pt, s_pa, r_pa, s_pb, r_pb, s_rw, r_rw, s_gz, r_gz, s_gx, r_gx,
):
    row = lax.axis_index("row")
    col = lax.axis_index("col")
    z, core = row // 2, row % 2
    x, y = col % NQ, col // NQ
    p = x + core * (y - x)
    q = y + core * (x - y)

    def at_pq(dp, dq):
        pp = lax.rem(p + dp + NQ, NQ)
        qq = lax.rem(q + dq + NQ, NQ)
        return (row, qq * (4 - 3 * core) + pp * (1 + 3 * core))

    def at_z(dz, dc):
        return (lax.rem(z + dz + NQ, NQ) * 2 + lax.rem(core + dc, 2), col)

    offsets_xy = [(dp, dq) for dq in range(NQ) for dp in range(NQ) if dp or dq]
    offsets_z = [(dz, dc) for dz in range(NQ) for dc in range(2) if dz or dc]
    sends = []

    def push(src, dst, s_sem, r_sem, device):
        copy = pltpu.make_async_remote_copy(
            src_ref=src, dst_ref=dst, send_sem=s_sem, recv_sem=r_sem, device_id=device, device_id_type=MESH
        )
        copy.start()
        sends.append(copy)

    def arrived(dst, s_sem, r_sem):
        pltpu.make_async_remote_copy(
            src_ref=dst, dst_ref=dst, send_sem=s_sem, recv_sem=r_sem, device_id=(row, col), device_id_type=MESH
        ).wait_recv()

    barrier = pltpu.get_barrier_semaphore()
    for dp, dq in offsets_xy:
        pl.semaphore_signal(barrier, inc=1, device_id=at_pq(dp, dq), device_id_type=MESH)
    for dz, dc in offsets_z:
        pl.semaphore_signal(barrier, inc=1, device_id=at_z(dz, dc), device_id_type=MESH)

    values = emb_ref[...].astype(F32)
    power = jnp.mean(values * values, axis=1, keepdims=True)
    unit = (values * lax.rsqrt(power + 1e-06) * (1.0 / math.sqrt(E))).astype(BF16)
    u_b[0, 0:NB, :] = unit[0:NB]
    u_a[0, 0:NA, :] = unit[NB:OWN]
    u_j[row] = unit
    start_all[row] = start_ref[...]
    acc[...] = jnp.zeros_like(acc)
    pl.semaphore_wait(barrier, len(offsets_xy) + len(offsets_z))

    def slot_a(dq, dp):
        return u_a.at[dq, pl.ds(dp * NA, NA)]

    def slot_b(dp, dq):
        return u_b.at[dp, pl.ds(dq * NB, NB)]

    def push_piece_a(dp):
        for dq in (1, 3):
            push(slot_a(0, dp), slot_a(dq, dp), s_a.at[dq, dp, 0], r_a.at[dq, dp, 0], at_pq(0, dq))

    def push_piece_b(dq):
        for dp in (1, 3):
            push(slot_b(0, dq), slot_b(dp, dq), s_b.at[dp, dq, 0], r_b.at[dp, dq, 0], at_pq(dp, 0))

    push(u_j.at[row], u_j.at[row], s_z.at[0, 1], r_z.at[0, 1], at_z(0, 1))
    for dz in (1, 3, 2):
        push(u_j.at[row], u_j.at[row], s_z.at[dz, 0], r_z.at[dz, 0], at_z(dz, 0))
    for d in (1, 3, 2):
        push(slot_a(0, 0), slot_a(0, d), s_a.at[0, d, 0], r_a.at[0, d, 0], at_pq(d, 0))
        push(slot_b(0, 0), slot_b(0, d), s_b.at[0, d, 0], r_b.at[0, d, 0], at_pq(0, d))
    push_piece_a(0)
    push_piece_b(0)

    def shard(dz, dc):
        return lax.rem(z - dz + NQ, NQ) * 2 + lax.rem(core + dc, 2)

    for d in (1, 3, 2):
        arrived(slot_a(0, d), s_a.at[0, d, 0], r_a.at[0, d, 0])
        push_piece_a(d)
        arrived(slot_b(0, d), s_b.at[0, d, 0], r_b.at[0, d, 0])
        push_piece_b(d)

    def tile(u_ref, t_ref, chunk, owner):
        rows_j = pl.ds(pl.multiple_of(owner * OWN, OWN), OWN)
        value = jnp.exp2(dot_nt(u_j[owner], u_ref[chunk]) * RATE)
        t_ref[chunk, rows_j, :] = value.astype(BF16)
        total = acc[rows_j, :]
        for lane in range(0, u_ref.shape[1], 128):
            total = total + value[:, lane : lane + 128]
        acc[rows_j, :] = total

    def tile_both(chunk, owner):
        tile(u_a, t_a, chunk, owner)
        tile(u_b, t_b, chunk, owner)

    def first(dz):
        def body(dc, carry):
            tile_both(0, shard(dz, dc))
            return carry

        lax.fori_loop(0, 2, body, 0)

    arrived(u_j.at[shard(0, 1)], s_z.at[0, 1], r_z.at[0, 1])
    first(0)
    for dz in (1, 3, 2):
        source = shard(dz, 0)
        arrived(u_j.at[source], s_z.at[dz, 0], r_z.at[dz, 0])
        push(u_j.at[source], u_j.at[source], s_z.at[dz, 1], r_z.at[dz, 1], at_z(0, 1))
        if dz == 2:
            for dz2, dc2 in offsets_z:
                push(start_all.at[row], start_all.at[row], s_st.at[dz2, dc2], r_st.at[dz2, dc2], at_z(dz2, dc2))
        arrived(u_j.at[shard(dz, 1)], s_z.at[dz, 1], r_z.at[dz, 1])
        first(dz)

    for d in range(NQ):
        for step, half in ((1, 0), (3, 1)):
            rows_a = pl.ds(d * NA + half * (NA // 2), NA // 2)
            rows_b = pl.ds(d * NB + half * (NB // 2), NB // 2)
            arrived(slot_a(step, d), s_a.at[step, d, 0], r_a.at[step, d, 0])
            push(u_a.at[step, rows_a], u_a.at[2, rows_a], s_a.at[2, d, half], r_a.at[2, d, half], at_pq(0, step))
            arrived(slot_b(step, d), s_b.at[step, d, 0], r_b.at[step, d, 0])
            push(u_b.at[step, rows_b], u_b.at[2, rows_b], s_b.at[2, d, half], r_b.at[2, d, half], at_pq(step, 0))

    def rest(chunk):
        def body(owner, carry):
            tile_both(chunk, owner)
            return carry

        lax.fori_loop(0, NZ, body, 0)

    rest(1)
    rest(3)
    for d in range(NQ):
        for half in range(2):
            rows_a = pl.ds(d * NA + half * (NA // 2), NA // 2)
            rows_b = pl.ds(d * NB + half * (NB // 2), NB // 2)
            arrived(u_a.at[2, rows_a], s_a.at[2, d, half], r_a.at[2, d, half])
            arrived(u_b.at[2, rows_b], s_b.at[2, d, half], r_b.at[2, d, half])
    rest(2)

    ones = jnp.ones((8, 128), BF16)
    for owner in range(NZ):
        rest_f32 = acc[owner * OWN : (owner + 1) * OWN, :]
        total = jnp.zeros((8, OWN), F32)
        for _ in range(3):
            piece = rest_f32.astype(BF16)
            rest_f32 = rest_f32 - piece.astype(F32)
            total = total + dot_nt(ones, piece)
        part_send[owner : owner + 1, :] = total[0:1, :]
    for dz, dc in offsets_z:
        push(part_send, part_recv.at[dz, dc], s_pt.at[dz, dc], r_pt.at[dz, dc], at_z(dz, dc))
    for dz, dc in offsets_z:
        arrived(start_all.at[shard(dz, dc)], s_st.at[dz, dc], r_st.at[dz, dc])
    for dz, dc in offsets_z:
        arrived(part_recv.at[dz, dc], s_pt.at[dz, dc], r_pt.at[dz, dc])
    degrees = part_send[...]
    for dz, dc in offsets_z:
        degrees = degrees + part_recv[dz, dc]
    part_recv[0, 0] = degrees
    scales = 1.0 / jnp.sqrt(degrees)
    scale_all[...] = scales
    deg_ref[...] = part_recv[0, 0, pl.ds(row, 1), :] * math.exp(-8.0)
    scale = scale_all[pl.ds(row, 1), :]

    for owner in range(NZ):
        lhs[:, owner * OWN : (owner + 1) * OWN] = (start_all[owner] * scales[owner : owner + 1, :]).astype(BF16)

    for step in range(ITERS):
        for chunk in (2, 1, 3, 0):
            out = jnp.dot(lhs[...], t_a[chunk], preferred_element_type=F32)
            for dp in range(NQ):
                block = out[:, dp * NA : (dp + 1) * NA]
                if dp or chunk:
                    send_a[step, chunk, dp] = block.astype(BF16)
                    push(send_a.at[step, chunk, dp], recv_a.at[step, chunk, dp], s_pa.at[step, chunk, dp],
                         r_pa.at[step, chunk, dp], at_pq(-dp, -chunk))
                else:
                    image_ref[:, NB:OWN] = block
            out = jnp.dot(lhs[...], t_b[chunk], preferred_element_type=F32)
            for dq in range(NQ):
                block = out[:, dq * NB : (dq + 1) * NB]
                if dq or chunk:
                    send_b[step, chunk, dq] = block.astype(BF16)
                    push(send_b.at[step, chunk, dq], recv_b.at[step, chunk, dq], s_pb.at[step, chunk, dq],
                         r_pb.at[step, chunk, dq], at_pq(-chunk, -dq))
                else:
                    image_ref[:, 0:NB] = block
        total_a = image_ref[:, NB:OWN]
        total_b = image_ref[:, 0:NB]
        for chunk in (2, 1, 3, 0):
            for d in range(NQ):
                if d or chunk:
                    arrived(recv_a.at[step, chunk, d], s_pa.at[step, chunk, d], r_pa.at[step, chunk, d])
                    total_a = total_a + recv_a[step, chunk, d].astype(F32)
                    arrived(recv_b.at[step, chunk, d], s_pb.at[step, chunk, d], r_pb.at[step, chunk, d])
                    total_b = total_b + recv_b[step, chunk, d].astype(F32)
        image_ref[:, NB:OWN] = total_a
        image_ref[:, 0:NB] = total_b
        image = image_ref[...] * scale
        gram = pack(dot_nt(image, image, HIGH))
        gram_z[step, 0, 0] = gram
        for dz, dc in offsets_z:
            push(gram_z.at[step, 0, 0], gram_z.at[step, dz, dc], s_gz.at[step, dz, dc], r_gz.at[step, dz, dc], at_z(dz, dc))
        if step + 1 < ITERS:
            raw_all[row] = image * scale
            for dz, dc in offsets_z:
                push(raw_all.at[row], raw_all.at[row], s_rw.at[dz, dc], r_rw.at[dz, dc], at_z(dz, dc))
        for dz, dc in offsets_z:
            arrived(gram_z.at[step, dz, dc], s_gz.at[step, dz, dc], r_gz.at[step, dz, dc])
            gram = gram + gram_z[step, dz, dc]
        gram_xy[step, 0, 0] = gram
        for dp, dq in offsets_xy:
            push(gram_xy.at[step, 0, 0], gram_xy.at[step, dq, dp], s_gx.at[step, dq, dp], r_gx.at[step, dq, dp], at_pq(dp, dq))
        for dp, dq in offsets_xy:
            arrived(gram_xy.at[step, dq, dp], s_gx.at[step, dq, dp], r_gx.at[step, dq, dp])
            gram = gram + gram_xy[step, dq, dp]
        inverse = inverse_factor(unpack(gram))
        if step + 1 < ITERS:
            for dz, dc in offsets_z:
                arrived(raw_all.at[shard(dz, dc)], s_rw.at[dz, dc], r_rw.at[dz, dc])
            for owner in range(NZ):
                lhs[:, owner * OWN : (owner + 1) * OWN] = jnp.dot(
                    inverse, raw_all[owner], precision=HIGH, preferred_element_type=F32
                ).astype(BF16)
        else:
            vec_ref[...] = jnp.dot(inverse, image, precision=HIGH, preferred_element_type=F32)

    for copy in sends:
        copy.wait_send()


def local(embeddings, start_vectors):
    dma = pltpu.SemaphoreType.DMA
    vmem = pltpu.VMEM
    pairs = []
    for shape in (
        (NQ, NQ, 2), (NQ, NQ, 2), (NQ, 2), (NQ, 2), (NQ, 2), (ITERS, NQ, NQ), (ITERS, NQ, NQ), (NQ, 2),
        (ITERS, NQ, 2), (ITERS, NQ, NQ),
    ):
        pairs += [dma(shape), dma(shape)]
    vectors, degrees = pl.pallas_call(
        kernel,
        out_shape=(jax.ShapeDtypeStruct((K, OWN), F32), jax.ShapeDtypeStruct((1, OWN), F32)),
        in_specs=[pl.BlockSpec(memory_space=vmem)] * 2,
        out_specs=(pl.BlockSpec(memory_space=vmem), pl.BlockSpec(memory_space=vmem)),
        scratch_shapes=[
            vmem((NQ, NQ * NA, E), BF16),
            vmem((NQ, NQ * NB, E), BF16),
            vmem((NZ, OWN, E), BF16),
            vmem((NQ, J, NQ * NA), BF16),
            vmem((NQ, J, NQ * NB), BF16),
            vmem((J, 128), F32),
            vmem((NZ, K, OWN), F32),
            vmem((NZ, OWN), F32),
            vmem((NQ, 2, NZ, OWN), F32),
            vmem((NZ, OWN), F32),
            vmem((K, J), BF16),
            vmem((ITERS, NQ, NQ, K, NA), BF16),
            vmem((ITERS, NQ, NQ, K, NB), BF16),
            vmem((ITERS, NQ, NQ, K, NA), BF16),
            vmem((ITERS, NQ, NQ, K, NB), BF16),
            vmem((NZ, K, OWN), F32),
            vmem((ITERS, NQ, 2, 8, 128), F32),
            vmem((ITERS, NQ, NQ, 8, 128), F32),
            vmem((K, OWN), F32),
            *pairs,
        ],
        compiler_params=pltpu.CompilerParams(
            collective_id=0, has_side_effects=True, vmem_limit_bytes=56 * 2**20
        ),
        name="subspace",
    )(embeddings, start_vectors)
    return (vectors, degrees.reshape(OWN))


def solution(mesh):
    return jax.shard_map(
        local,
        mesh=mesh,
        in_specs=(P(("row", "col"), None), P(None, ("row", "col"))),
        out_specs=(P(None, ("row", "col")), P(("row", "col"))),
        check_vma=False,
    )
```

time: 555 us -> 88.7 us (0.16)
  blocking collectives: 232 us -> 0 us
  waiting for transfers between devices: 208 us -> 0 us
  Pallas kernels: 0 us -> 85.2 us
  matrix products: 66.3 us -> 0 us
  other arithmetic: 25.6 us -> 0.6 us
  between operations: 14.5 us -> 0.65 us
    unnamed x6 -> x0, waiting for transfers between devices: 135 us -> none
    psum x2 -> x0, blocking collectives: 132 us -> none  [local(): gram = lax.psum(local_gram, ('row', 'col'))]
    pallas_call x0 -> x1, Pallas kernels: none -> 85.2 us  [local(): pl.pallas_call(kernel, out_shape=(jax.ShapeDtypeStruct((K, OWN), F32), ja...]
    all_gather x2 -> x0, waiting for transfers between devices: 72.9 us -> none  [the longest x1 47.5 us: local(): row_emb = lax.all_gather(own_unit, 'col', axis=0, tiled=True)]
    dot_general x14 -> x0, matrix products: 65.1 us -> none  [the longest x10 39.4 us: one_piece(): lax.dot_general(piece, col_emb, (((1,), (1,)), ((), ())), preferred_eleme...]
    unnamed x1 -> x0, blocking collectives: 58.2 us -> none
    all_gather x2 -> x0, blocking collectives: 41.8 us -> none  [local(): lax.all_gather(scaled, 'row', axis=1, tiled=True)]
    another operation x10 -> x0, other arithmetic: 13.4 us -> none  [the longest x6 7.19 us: local(): lower = jnp.linalg.cholesky(gram)]
  transfers between devices with their start and end apart: 4 -> 0, of which waited for: 4 -> 0; matrix products, arithmetic and copies ran while one was open for 0% -> 0% of each run, Pallas kernels for 0% -> 0%
where the time goes in v1:
time: 88.7 us; the launch traced here: 88.5 us
  Pallas kernels  85.2 us (96%)
  local copies, waits for them, and re-layouts  2.08 us (2%)
    pallas_call x1, Pallas kernels, local(): pl.pallas_call(kernel, out_shape=(jax.ShapeDtypeStruct((K, OWN), F32), ja...  85.2 us
    unnamed x3, local copies, waits for them, and re-layouts  2.08 us

profile of v1, /device:TPU:1, one launch (start us, length us, event | category | flops | bytes accessed | tf_op | source)
XLA Modules:
  0.0 88.5 jit_solution(7523202687303506399)
XLA Ops:
  0.6 85.2 %subspace.1 = (f32[32,320]{1,0:T(8,128)}, f32[1,320]{1,0:T(1,128)}) custom-call(bf16[320,256]{1,0:T(8,128)(2,1)} %emb_ref.1, f32[32,320]{1,0:T(8,128)} %start_ref.1), custom_call_target="tpu_custom_call" | custom-call | tf_op jit(solution)/shard_map/subspace/pallas_call | solution.py:298
  85.8 0.0 copy-start
  85.8 0.7 copy-done
  86.5 0.6 reduce
  87.1 1.4 %copy.5 = f32[32,320]{1,0:T(8,128)} copy(f32[32,320]{1,0:T(8,128)} %get-tuple-element.8) | data formatting | bytes 81920
Async XLA Ops:
  85.8 0.7 copy-start

commit v2 on v0

v2 whole, which is shorter than its diff:
```python
import math

import jax
import jax.numpy as jnp
from jax import lax
from jax.experimental import pallas as pl
from jax.experimental.pallas import tpu as pltpu
from jax.sharding import PartitionSpec as P

K = 32
E = 256
OWN = 320
HALF = OWN // 2
NZ = 8
NQ = 4
J = NZ * OWN
PAIR = 2 * OWN
WIDE = NQ * OWN
RATE = 8.0 / math.log(2.0)
MESH = pl.DeviceIdType.MESH
HIGH = lax.Precision.HIGHEST
F32 = jnp.float32
BF16 = jnp.bfloat16
ORDER = (
    (0, 0), (1, 0), (3, 0), (0, 1),
    (0, 3), (2, 0), (0, 2), (1, 1),
    (1, 3), (3, 1), (3, 3), (1, 2),
    (3, 2), (2, 1), (2, 3), (2, 2),
)
SLOT = {place: slot for slot, place in enumerate(ORDER)}


def dot_nt(a, b, precision=None):
    return lax.dot_general(a, b, (((1,), (1,)), ((), ())), precision=precision, preferred_element_type=F32)


def pack(square):
    return jnp.concatenate([square[8 * b : 8 * b + 8, :] for b in range(4)], axis=1)


def unpack(packed):
    return jnp.concatenate([packed[:, K * b : K * b + K] for b in range(4)], axis=0)


def inverse_factor(gram):
    rows = lax.broadcasted_iota(jnp.int32, (K, K), 0)
    columns = lax.broadcasted_iota(jnp.int32, (K, K), 1)
    eye = (rows == columns).astype(F32)
    work = jnp.concatenate([gram, eye], axis=1)
    below = lax.broadcasted_iota(jnp.int32, (K, 1), 0)
    pivots = jnp.ones((K, 1), F32)
    for k in range(K):
        pivot = work[k : k + 1, k : k + 1]
        column = work[:, k : k + 1]
        factor = jnp.where(below > k, column / pivot, 0.0)
        pivots = jnp.where(below == k, pivot, pivots)
        work = work - factor * work[k : k + 1, :]
    return work[:, K : 2 * K] * (1.0 / jnp.sqrt(pivots))


def kernel(
    emb_ref, start_ref, vec_ref, deg_ref,
    u_i, u_j, tiles, acc, start_all, part, scale_all, lhs, lhs_pair, out_acc,
    send_1, recv_1, send_2, recv_2, raw_all, gram_z, gram_xy,
    s_i, r_i, s_j, r_j, s_st, r_st, s_pt, r_pt, s_1, r_1, s_2, r_2, s_rw, r_rw, s_gz, r_gz, s_gx, r_gx,
):
    row = lax.axis_index("row")
    col = lax.axis_index("col")
    z, core = row // 2, row % 2
    x, y = col % NQ, col // NQ
    p = x + core * (y - x)
    q = y + core * (x - y)

    def at_pq(dp, dq):
        pp = lax.rem(p + dp + NQ, NQ)
        qq = lax.rem(q + dq + NQ, NQ)
        return (row, qq * (4 - 3 * core) + pp * (1 + 3 * core))

    def shard(dz, dc):
        return lax.rem(z - dz + NQ, NQ) * 2 + lax.rem(core + dc, 2)

    def at_z(dz, dc):
        return (shard(-dz % NQ, dc), col)

    offsets_z = [(dz, dc) for dz in range(NQ) for dc in range(2) if dz or dc]
    sibling = at_z(0, 1)

    def push(src, dst, s_sem, r_sem, device):
        pltpu.make_async_remote_copy(
            src_ref=src, dst_ref=dst, send_sem=s_sem, recv_sem=r_sem, device_id=device, device_id_type=MESH
        ).start()

    def arrived(ref, r_sem):
        pltpu.make_async_remote_copy(
            src_ref=ref, dst_ref=ref, send_sem=r_sem, recv_sem=r_sem, device_id=sibling, device_id_type=MESH
        ).wait_recv()

    def sent(ref, s_sem):
        pltpu.make_async_remote_copy(
            src_ref=ref, dst_ref=ref, send_sem=s_sem, recv_sem=s_sem, device_id=sibling, device_id_type=MESH
        ).wait_send()

    barrier = pltpu.get_barrier_semaphore()
    neighbours = [at_pq(1, 0), at_pq(3, 0), at_pq(0, 1), at_pq(0, 3), at_z(1, 0), at_z(3, 0), sibling]
    for device in neighbours:
        pl.semaphore_signal(barrier, inc=1, device_id=device, device_id_type=MESH)

    values = emb_ref[...].astype(F32)
    power = jnp.mean(values * values, axis=1, keepdims=True)
    unit = (values * lax.rsqrt(power + 1e-06) * (1.0 / math.sqrt(E))).astype(BF16)
    u_i[0] = unit
    u_j[row] = unit
    start_all[row] = start_ref[...]
    acc[...] = jnp.zeros_like(acc)
    pl.semaphore_wait(barrier, len(neighbours))

    def piece(source, target, device):
        push(u_i.at[SLOT[source]], u_i.at[SLOT[target]], s_i, r_i.at[SLOT[target]], device)

    def half_piece(source, target, half, device):
        rows = pl.ds(half * HALF, HALF)
        push(u_i.at[SLOT[source], rows], u_i.at[SLOT[target], rows], s_i, r_i.at[SLOT[target]], device)

    def here(place):
        arrived(u_i.at[SLOT[place]], r_i.at[SLOT[place]])

    def second_ring(d):
        piece((d, 0), (d, 1), at_pq(0, 1))
        piece((d, 0), (d, 3), at_pq(0, 3))

    def on_first(d):
        here((d, 0))
        half_piece((d, 0), (2, 0), 0 if d == 1 else 1, at_pq(d, 0))
        second_ring(d)

    def on_second(d, e):
        here((d, e))
        half_piece((d, e), (d, 2), 0 if e == 1 else 1, at_pq(0, e))

    def shard_push(dz, device, sem):
        push(u_j.at[shard(dz, 0)], u_j.at[shard(dz, 0)], s_j, sem, device)

    def on_z(dz):
        source = shard(dz, 0)
        arrived(u_j.at[source], r_j.at[dz, 0])
        shard_push(dz, sibling, r_j.at[dz, 1])
        if dz != 2:
            rows = pl.ds(0 if dz == 1 else HALF, HALF)
            push(u_j.at[source, rows], u_j.at[source, rows], s_j, r_j.at[2, 0], at_z(dz, 0))

    def tile(chunk, owner):
        rows_j = pl.ds(pl.multiple_of(owner * OWN, OWN), OWN)
        block = u_i[NQ * chunk : NQ * chunk + NQ].reshape(WIDE, E)
        value = jnp.exp2(dot_nt(u_j[owner], block) * RATE)
        tiles[chunk, rows_j, :] = value.astype(BF16)
        total = acc[rows_j, :]
        for lane in range(0, WIDE, 128):
            total = total + value[:, lane : lane + 128]
        acc[rows_j, :] = total

    def tile_pair(chunk, dz):
        arrived(u_j.at[shard(dz, 1)], r_j.at[dz, 1])

        def body(dc, carry):
            tile(chunk, shard(dz, dc))
            return carry

        lax.fori_loop(0, 2, body, 0)

    def tile_range(chunk, first, last):
        def body(owner, carry):
            tile(chunk, owner)
            return carry

        lax.fori_loop(first, last, body, 0)

    shard_push(0, sibling, r_j.at[0, 1])
    piece((0, 0), (1, 0), at_pq(1, 0))
    piece((0, 0), (3, 0), at_pq(3, 0))
    shard_push(0, at_z(1, 0), r_j.at[1, 0])
    shard_push(0, at_z(3, 0), r_j.at[3, 0])
    second_ring(0)
    on_first(1)
    on_first(3)
    on_second(0, 1)
    on_second(0, 3)
    on_z(1)
    on_z(3)
    tile_pair(0, 0)
    tile_pair(0, 1)
    here((2, 0))
    second_ring(2)
    tile_pair(0, 3)
    on_second(1, 1)
    on_second(1, 3)
    on_z(2)
    for dz, dc in offsets_z:
        push(start_all.at[row], start_all.at[row], s_st, r_st, at_z(dz, dc))
    tile_pair(0, 2)
    on_second(3, 1)
    on_second(3, 3)
    here((0, 2))
    tile_range(1, 0, NZ // 2)
    on_second(2, 1)
    on_second(2, 3)
    tile_range(1, NZ // 2, NZ)
    here((1, 2))
    tile_range(2, 0, NZ)
    here((3, 2))
    here((2, 2))
    tile_range(3, 0, NZ)
    arrived(start_all.at[0:7], r_st)

    ones = jnp.ones((8, 128), BF16)
    for owner in range(NZ):
        left = acc[owner * OWN : (owner + 1) * OWN, :]
        total = jnp.zeros((8, OWN), F32)
        for _ in range(3):
            top = left.astype(BF16)
            left = left - top.astype(F32)
            total = total + dot_nt(ones, top)
        part[0, owner : owner + 1, :] = total[0:1, :]
    for dz, dc in offsets_z:
        push(part.at[0], part.at[2 * dz + dc], s_pt, r_pt, at_z(dz, dc))
    arrived(part.at[1:8], r_pt)
    degrees = part[0]
    for slot in range(1, NZ):
        degrees = degrees + part[slot]
    scales = 1.0 / jnp.sqrt(degrees)
    scale_all[0] = scales
    scale_all[1] = degrees * math.exp(-8.0)
    deg_ref[...] = scale_all[1, pl.ds(row, 1), :]
    scale = scale_all[0, pl.ds(row, 1), :]
    for owner in range(NZ):
        lhs[:, owner * OWN : (owner + 1) * OWN] = (start_all[owner] * scales[owner : owner + 1, :]).astype(BF16)

    def scatter(chunk, out, send, recv, s_sem, r_sem):
        for sub in range(NQ):
            slot = NQ * chunk + sub
            block = out[:, sub * OWN : (sub + 1) * OWN]
            if slot == 0:
                return_own = block
                continue
            send[slot] = block.astype(send.dtype)
            dp, dq = ORDER[slot]
            push(send.at[slot], recv.at[slot], s_sem, r_sem, at_pq(-dp, -dq))
        return return_own if chunk == 0 else None

    def gathered(own, recv, r_sem):
        arrived(recv.at[1:16], r_sem)
        for slot in range(1, NQ * NQ):
            own = own + recv[slot].astype(F32)
        return own * scale

    for chunk in (3, 2, 1, 0):
        own = scatter(chunk, jnp.dot(lhs[...], tiles[chunk], preferred_element_type=F32), send_1, recv_1, s_1, r_1)
    image = gathered(own, recv_1, r_1)

    raw = image * scale
    high = raw.astype(BF16)
    raw_all[row, 0:K, :] = high
    raw_all[row, K : 2 * K, :] = (raw - high.astype(F32)).astype(BF16)

    def raw_push(dz, device, sem):
        push(raw_all.at[shard(dz, 0)], raw_all.at[shard(dz, 0)], s_rw, sem, device)

    raw_push(0, sibling, r_rw.at[0, 1])
    for dz in (2, 1, 3):
        raw_push(0, at_z(dz, 0), r_rw.at[dz, 0])

    def gram_start(step, image):
        gram_z[step, 0] = pack(dot_nt(image, image, HIGH))
        for dz, dc in offsets_z:
            push(gram_z.at[step, 0], gram_z.at[step, 2 * dz + dc], s_gz.at[step], r_gz.at[step], at_z(dz, dc))

    def gram_middle(step):
        arrived(gram_z.at[step, 1:8], r_gz.at[step])
        gram = gram_z[step, 0]
        for slot in range(1, NZ):
            gram = gram + gram_z[step, slot]
        gram_xy[step, 0] = gram
        for slot in range(1, NQ * NQ):
            dp, dq = ORDER[slot]
            push(gram_xy.at[step, 0], gram_xy.at[step, slot], s_gx.at[step], r_gx.at[step], at_pq(dp, dq))

    def gram_end(step):
        arrived(gram_xy.at[step, 1:16], r_gx.at[step])
        gram = gram_xy[step, 0]
        for slot in range(1, NQ * NQ):
            gram = gram + gram_xy[step, slot]
        return inverse_factor(unpack(gram))

    gram_start(0, image)

    def product(dz, chunk):
        first = lax.rem(z - dz + NQ, NQ) * 2
        rows = pl.ds(pl.multiple_of(first * OWN, PAIR), PAIR)
        out = jnp.dot(lhs_pair[...], tiles[chunk, rows, :], preferred_element_type=F32)
        return out[0:K] + out[K : 2 * K]

    for dz in (0, 1, 3, 2):
        first = lax.rem(z - dz + NQ, NQ) * 2
        if dz:
            arrived(raw_all.at[shard(dz, 0)], r_rw.at[dz, 0])
            raw_push(dz, sibling, r_rw.at[dz, 1])
        if dz == 1:
            gram_middle(0)
        arrived(raw_all.at[shard(dz, 1)], r_rw.at[dz, 1])
        lhs_pair[:, 0:OWN] = raw_all[first]
        lhs_pair[:, OWN:PAIR] = raw_all[first + 1]
        for chunk in (3, 2, 1, 0):
            out = product(dz, chunk)
            if dz == 0:
                out_acc[chunk] = out
            elif dz != 2:
                out_acc[chunk] += out
            else:
                own = scatter(chunk, out_acc[chunk] + out, send_2, recv_2, s_2, r_2)
    inverse = gram_end(0)
    image = gathered(own, recv_2, r_2)
    image = jnp.dot(inverse, image, precision=HIGH, preferred_element_type=F32)
    gram_start(1, image)
    gram_middle(1)
    inverse = gram_end(1)
    vec_ref[...] = jnp.dot(inverse, image, precision=HIGH, preferred_element_type=F32)

    sent(u_i.at[0:15], s_i)
    sent(u_j.at[0:7], s_j)
    sent(start_all.at[0:7], s_st)
    sent(part.at[1:8], s_pt)
    sent(send_1.at[1:16], s_1)
    sent(raw_all.at[0:7], s_rw)
    sent(send_2.at[1:16], s_2)
    for step in range(2):
        sent(gram_z.at[step, 1:8], s_gz.at[step])
        sent(gram_xy.at[step, 1:16], s_gx.at[step])


def local(embeddings, start_vectors):
    dma = pltpu.SemaphoreType.DMA
    vmem = pltpu.VMEM
    vectors, degrees = pl.pallas_call(
        kernel,
        out_shape=(jax.ShapeDtypeStruct((K, OWN), F32), jax.ShapeDtypeStruct((1, OWN), F32)),
        in_specs=[pl.BlockSpec(memory_space=vmem)] * 2,
        out_specs=(pl.BlockSpec(memory_space=vmem), pl.BlockSpec(memory_space=vmem)),
        scratch_shapes=[
            vmem((NQ * NQ, OWN, E), BF16),
            vmem((NZ, OWN, E), BF16),
            vmem((NQ, J, WIDE), BF16),
            vmem((J, 128), F32),
            vmem((NZ, K, OWN), F32),
            vmem((NZ, NZ, OWN), F32),
            vmem((2, NZ, OWN), F32),
            vmem((K, J), BF16),
            vmem((2 * K, PAIR), BF16),
            vmem((NQ, K, WIDE), F32),
            vmem((NQ * NQ, K, OWN), BF16),
            vmem((NQ * NQ, K, OWN), BF16),
            vmem((NQ * NQ, K, OWN), F32),
            vmem((NQ * NQ, K, OWN), F32),
            vmem((NZ, 2 * K, OWN), BF16),
            vmem((2, NZ, 8, 128), F32),
            vmem((2, NQ * NQ, 8, 128), F32),
            dma, dma((NQ * NQ,)),
            dma, dma((NQ, 2)),
            dma, dma,
            dma, dma,
            dma, dma,
            dma, dma,
            dma, dma((NQ, 2)),
            dma((2,)), dma((2,)),
            dma((2,)), dma((2,)),
        ],
        compiler_params=pltpu.CompilerParams(
            collective_id=0, has_side_effects=True, vmem_limit_bytes=56 * 2**20
        ),
        name="subspace",
    )(embeddings, start_vectors)
    return (vectors, degrees.reshape(OWN))


def solution(mesh):
    return jax.shard_map(
        local,
        mesh=mesh,
        in_specs=(P(("row", "col"), None), P(None, ("row", "col"))),
        out_specs=(P(None, ("row", "col")), P(("row", "col"))),
        check_vma=False,
    )
```

time: 555 us -> 82.7 us (0.15)
  blocking collectives: 232 us -> 0 us
  waiting for transfers between devices: 208 us -> 0 us
  Pallas kernels: 0 us -> 79.2 us
  matrix products: 66.3 us -> 0 us
  other arithmetic: 25.6 us -> 0.6 us
  between operations: 14.5 us -> 0.65 us
    unnamed x6 -> x0, waiting for transfers between devices: 135 us -> none
    psum x2 -> x0, blocking collectives: 132 us -> none  [local(): gram = lax.psum(local_gram, ('row', 'col'))]
    pallas_call x0 -> x1, Pallas kernels: none -> 79.2 us  [local(): pl.pallas_call(kernel, out_shape=(jax.ShapeDtypeStruct((K, OWN), F32), ja...]
    all_gather x2 -> x0, waiting for transfers between devices: 72.9 us -> none  [the longest x1 47.5 us: local(): row_emb = lax.all_gather(own_unit, 'col', axis=0, tiled=True)]
    dot_general x14 -> x0, matrix products: 65.1 us -> none  [the longest x10 39.4 us: one_piece(): lax.dot_general(piece, col_emb, (((1,), (1,)), ((), ())), preferred_eleme...]
    unnamed x1 -> x0, blocking collectives: 58.2 us -> none
    all_gather x2 -> x0, blocking collectives: 41.8 us -> none  [local(): lax.all_gather(scaled, 'row', axis=1, tiled=True)]
    another operation x10 -> x0, other arithmetic: 13.4 us -> none  [the longest x6 7.19 us: local(): lower = jnp.linalg.cholesky(gram)]
  transfers between devices with their start and end apart: 4 -> 0, of which waited for: 4 -> 0; matrix products, arithmetic and copies ran while one was open for 0% -> 0% of each run, Pallas kernels for 0% -> 0%
where the time goes in v2:
time: 82.7 us; the launch traced here: 82.5 us
  Pallas kernels  79.2 us (96%)
  local copies, waits for them, and re-layouts  2.08 us (3%)
    pallas_call x1, Pallas kernels, local(): pl.pallas_call(kernel, out_shape=(jax.ShapeDtypeStruct((K, OWN), F32), ja...  79.2 us
    unnamed x3, local copies, waits for them, and re-layouts  2.08 us

profile of v2, /device:TPU:1, one launch (start us, length us, event | category | flops | bytes accessed | tf_op | source)
XLA Modules:
  0.0 82.5 jit_solution(627234432320667778)
XLA Ops:
  0.6 79.2 %subspace.1 = (f32[32,320]{1,0:T(8,128)}, f32[1,320]{1,0:T(1,128)}) custom-call(bf16[320,256]{1,0:T(8,128)(2,1)} %emb_ref.1, f32[32,320]{1,0:T(8,128)} %start_ref.1), custom_call_target="tpu_custom_call" | custom-call | tf_op jit(solution)/shard_map/subspace/pallas_call | solution.py:342
  79.8 0.0 copy-start
  79.8 0.7 copy-done
  80.5 0.6 reduce
  81.1 1.4 %copy.5 = f32[32,320]{1,0:T(8,128)} copy(f32[32,320]{1,0:T(8,128)} %get-tuple-element.8) | data formatting | bytes 81920
Async XLA Ops:
  79.8 0.7 copy-start

commit v3 on v0

v3 whole, which is shorter than its diff:
```python
import math

import jax
import jax.numpy as jnp
from jax import lax
from jax.experimental import pallas as pl
from jax.experimental.pallas import tpu as pltpu
from jax.sharding import PartitionSpec as P

K = 32
PLACES = ((0, 0), (0, 1), (1, 0), (3, 0), (2, 0), (1, 1), (3, 1), (2, 1))
E = 256
OWN = 320
HALF = OWN // 2
NZ = 8
NQ = 4
J = NZ * OWN
PAIR = 2 * OWN
WIDE = NQ * OWN
RATE = 8.0 / math.log(2.0)
MESH = pl.DeviceIdType.MESH
HIGH = lax.Precision.HIGHEST
F32 = jnp.float32
BF16 = jnp.bfloat16


def dot_nt(a, b, precision=None):
    return lax.dot_general(a, b, (((1,), (1,)), ((), ())), precision=precision, preferred_element_type=F32)


def pack(square):
    return jnp.concatenate([square[8 * b : 8 * b + 8, :] for b in range(4)], axis=1)


def unpack(packed):
    return jnp.concatenate([packed[:, K * b : K * b + K] for b in range(4)], axis=0)


def inverse_factor(gram):
    rows = lax.broadcasted_iota(jnp.int32, (K, K), 0)
    columns = lax.broadcasted_iota(jnp.int32, (K, K), 1)
    eye = (rows == columns).astype(F32)
    work = jnp.concatenate([gram, eye], axis=1)
    below = lax.broadcasted_iota(jnp.int32, (K, 1), 0)
    pivots = jnp.ones((K, 1), F32)
    for k in range(K):
        pivot = work[k : k + 1, k : k + 1]
        column = work[:, k : k + 1]
        factor = jnp.where(below > k, column / pivot, 0.0)
        pivots = jnp.where(below == k, pivot, pivots)
        work = work - factor * work[k : k + 1, :]
    return work[:, K : 2 * K] * (1.0 / jnp.sqrt(pivots))


def kernel(
    emb_ref, start_ref, vec_ref, deg_ref,
    u_i, u_j, tiles, acc, start_all, part, scale_all, lhs, lhs_pair, out_acc,
    sib_send, sib_recv, sum_send, sum_recv, raw_all, gram_c, gram_r,
    s_i, r_i, s_j, r_j, s_st, r_st, s_pt, r_pt, s_sb, r_sb, s_sm, r_sm, s_rw, r_rw, s_gc, r_gc, s_gr, r_gr,
):
    row = lax.axis_index("row")
    col = lax.axis_index("col")
    z, core = row // 2, row % 2
    x, y = col % NQ, col // NQ
    y_rows = y + 1 - 2 * (y % 2)
    y_cols = NQ - 1 - y
    sibling = (z * 2 + 1 - core, col)

    def at_r(dx, dy, dc=0):
        place = (y_rows if dy else y) * NQ + lax.rem(x + dx + NQ, NQ)
        return (z * 2 + (1 - core if dc else core), place)

    def at_c(dz, dy):
        return (lax.rem(z + dz + NQ, NQ) * 2 + core, (y_cols if dy else y) * NQ + x)

    def j_slot(dz, dy):
        return lax.rem(z - dz + NQ, NQ) * 2 + (y // 2) + dy * (1 - 2 * (y // 2))

    offsets_c = [(dz, dy) for dz, dy in PLACES if dz or dy]
    offsets_r = [(dx, dy, dc) for dx, dy in PLACES for dc in range(2) if dx or dy or dc]
    mine = j_slot(0, 0)

    def push(src, dst, s_sem, r_sem, device):
        pltpu.make_async_remote_copy(
            src_ref=src, dst_ref=dst, send_sem=s_sem, recv_sem=r_sem, device_id=device, device_id_type=MESH
        ).start()

    def arrived(ref, r_sem):
        pltpu.make_async_remote_copy(
            src_ref=ref, dst_ref=ref, send_sem=r_sem, recv_sem=r_sem, device_id=sibling, device_id_type=MESH
        ).wait_recv()

    def sent(ref, s_sem):
        pltpu.make_async_remote_copy(
            src_ref=ref, dst_ref=ref, send_sem=s_sem, recv_sem=s_sem, device_id=sibling, device_id_type=MESH
        ).wait_send()

    barrier = pltpu.get_barrier_semaphore()
    neighbours = [at_r(1, 0), at_r(3, 0), at_r(0, 1), at_c(1, 0), at_c(3, 0), at_c(0, 1), sibling]
    for device in neighbours:
        pl.semaphore_signal(barrier, inc=1, device_id=device, device_id_type=MESH)

    values = emb_ref[...].astype(F32)
    power = jnp.mean(values * values, axis=1, keepdims=True)
    unit = (values * lax.rsqrt(power + 1e-06) * (1.0 / math.sqrt(E))).astype(BF16)
    u_i[0] = unit
    u_j[mine] = unit
    start_all[mine] = start_ref[...]
    acc[...] = jnp.zeros_like(acc)
    pl.semaphore_wait(barrier, len(neighbours))

    def i_slot(dx, dy, dc=0):
        return 2 * PLACES.index((dx % NQ, dy)) + dc

    def row_piece(dx, dy, step, flip, half=None):
        rows = pl.ds(0, OWN) if half is None else pl.ds(half * HALF, HALF)
        to = i_slot(dx + step, dy ^ flip)
        push(u_i.at[i_slot(dx, dy), rows], u_i.at[to, rows], s_i, r_i.at[to], at_r(step, flip))

    def row_over(dx, dy):
        push(u_i.at[i_slot(dx, dy)], u_i.at[i_slot(dx, dy, 1)], s_i, r_i.at[i_slot(dx, dy, 1)], sibling)

    def row_here(dx, dy, dc=0):
        arrived(u_i.at[i_slot(dx, dy, dc)], r_i.at[i_slot(dx, dy, dc)])

    def col_piece(dz, dy, step, flip, half=None):
        rows = pl.ds(0, OWN) if half is None else pl.ds(half * HALF, HALF)
        slot = j_slot(dz, dy)
        push(u_j.at[slot, rows], u_j.at[slot, rows], s_j, r_j.at[(dz + step) % NQ, dy ^ flip], at_c(step, flip))

    def col_over(dz, dy):
        pass

    def col_here(dz, dy):
        arrived(u_j.at[j_slot(dz, dy)], r_j.at[dz, dy])

    def event(here, piece, over, d, dy):
        here(d, dy)
        if d in (1, 3) and dy == 0:
            piece(d, 0, d, 0, 0 if d == 1 else 1)
            pl.when(core == 1)(lambda: piece(d, 0, 0, 1))
        elif (d, dy) == (0, 1):

            @pl.when(core == 0)
            def _():
                piece(0, 1, 1, 0)
                piece(0, 1, 3, 0)

        elif (d, dy) == (2, 0):
            pl.when(core == 1)(lambda: piece(2, 0, 0, 1))
        elif d in (1, 3):
            pl.when(core == 0)(lambda: piece(d, 1, d, 0, 0 if d == 1 else 1))
        over(d, dy)

    def on_row(dx, dy):
        event(row_here, row_piece, row_over, dx, dy)

    def on_col(dz, dy):
        event(col_here, col_piece, col_over, dz, dy)

    def tile(chunk, slot):
        rows_j = pl.ds(pl.multiple_of(slot * OWN, OWN), OWN)
        block = u_i[pl.ds(NQ * chunk, NQ)].reshape(WIDE, E)
        value = jnp.exp2(dot_nt(u_j[slot], block) * RATE)
        tiles[chunk, rows_j, :] = value.astype(BF16)
        total = acc[rows_j, :]
        for lane in range(0, WIDE, 128):
            total = total + value[:, lane : lane + 128]
        acc[rows_j, :] = total

    def tile_range(first, last, count, place):
        def body(n, carry):
            tile(first + lax.rem(n, last - first), j_slot(*place(n // (last - first))))
            return carry

        lax.fori_loop(0, count * (last - first), body, 0)

    def near(n):
        return (n // 2) * (2 * (n % 2) + 1), (1 - n // 2) * (n % 2)

    def beside(n):
        return 2 * n + 1, 1

    row_over(0, 0)
    for piece in (row_piece, col_piece):
        piece(0, 0, 0, 1)
        piece(0, 0, 1, 0)
        piece(0, 0, 3, 0)
    for place in PLACES[1:4]:
        on_row(*place)
        on_col(*place)
    for dx, dy in PLACES[0:2]:
        row_here(dx, dy, 1)
    tile_range(0, 1, 4, near)
    for dx, dy in PLACES[2:4]:
        row_here(dx, dy, 1)
    on_row(2, 0)
    on_col(2, 0)
    tile_range(1, 2, 4, near)
    for place in PLACES[5:7]:
        on_row(*place)
        on_col(*place)
    tile_range(0, 2, 2, beside)
    row_here(2, 0, 1)
    row_here(1, 1, 1)
    tile_range(2, 3, 4, near)
    on_col(2, 1)
    for dz, dy in offsets_c:
        push(start_all.at[mine], start_all.at[mine], s_st, r_st, at_c(dz, dy))
    on_row(2, 1)
    tile_range(2, 3, 2, beside)
    row_here(3, 1, 1)
    row_here(2, 1, 1)
    tile_range(3, 4, 4, near)
    tile_range(3, 4, 2, beside)
    tile_range(0, 4, 2, lambda n: (2, n))
    arrived(start_all.at[0:7], r_st)

    ones = jnp.ones((8, 128), BF16)
    for slot in range(NZ):
        left = acc[slot * OWN : (slot + 1) * OWN, :]
        total = jnp.zeros((8, OWN), F32)
        for _ in range(3):
            top = left.astype(BF16)
            left = left - top.astype(F32)
            total = total + dot_nt(ones, top)
        part[0, slot : slot + 1, :] = total[0:1, :]
    for n, (dz, dy) in enumerate(offsets_c):
        push(part.at[0], part.at[n + 1], s_pt, r_pt, at_c(dz, dy))
    arrived(part.at[1:8], r_pt)
    degrees = part[0]
    for n in range(1, NZ):
        degrees = degrees + part[n]
    scales = 1.0 / jnp.sqrt(degrees)
    scale_all[0] = scales
    scale_all[1] = degrees * math.exp(-8.0)
    deg_ref[...] = scale_all[1, pl.ds(mine, 1), :]
    scale = scale_all[0, pl.ds(mine, 1), :]
    for slot in range(NZ):
        lhs[:, slot * OWN : (slot + 1) * OWN] = (start_all[slot] * scales[slot : slot + 1, :]).astype(BF16)

    def to_sibling(step, chunk, out):
        pair = pl.ds(2 * chunk, 2)
        for sub in range(2):
            sum_send[step, 2 * chunk + sub] = out[:, sub * PAIR : sub * PAIR + OWN]
            sib_send[step, 2 * chunk + sub] = out[:, sub * PAIR + OWN : (sub + 1) * PAIR]
        push(sib_send.at[step, pair], sib_recv.at[step, pair], s_sb.at[step], r_sb.at[step, chunk], sibling)

    def to_owners(step, chunk):
        arrived(sib_recv.at[step, pl.ds(2 * chunk, 2)], r_sb.at[step, chunk])
        for n in (2 * chunk + 1, 2 * chunk):
            dx, dy = PLACES[n]
            sum_send[step, n] += sib_recv[step, n]
            if n:
                push(sum_send.at[step, n], sum_recv.at[step, n], s_sm.at[step], r_sm.at[step], at_r(-dx, dy))

    def gathered(step):
        arrived(sum_recv.at[step, 1:8], r_sm.at[step])
        total = sum_send[step, 0]
        for n in range(1, NZ):
            total = total + sum_recv[step, n]
        return total * scale

    for chunk in (3, 2, 1, 0):
        to_sibling(0, chunk, jnp.dot(lhs[...], tiles[chunk], preferred_element_type=F32))
        if chunk < 3:
            to_owners(0, chunk + 1)
    to_owners(0, 0)
    image = gathered(0)

    raw = image * scale
    high = raw.astype(BF16)
    raw_all[mine, 0:K, :] = high
    raw_all[mine, K : 2 * K, :] = (raw - high.astype(F32)).astype(BF16)
    for dz, dy in ((0, 1), (1, 1), (3, 1), (2, 1), (2, 0), (1, 0), (3, 0)):
        push(raw_all.at[mine], raw_all.at[mine], s_rw, r_rw.at[dz, dy], at_c(dz, dy))

    def gram_start(step, image):
        gram_c[step, 0] = pack(dot_nt(image, image, HIGH))
        for n, (dz, dy) in enumerate(offsets_c):
            push(gram_c.at[step, 0], gram_c.at[step, n + 1], s_gc.at[step], r_gc.at[step], at_c(dz, dy))

    def gram_middle(step):
        arrived(gram_c.at[step, 1:8], r_gc.at[step])
        gram = gram_c[step, 0]
        for n in range(1, NZ):
            gram = gram + gram_c[step, n]
        gram_r[step, 0] = gram
        for n, (dx, dy, dc) in enumerate(offsets_r):
            push(gram_r.at[step, 0], gram_r.at[step, n + 1], s_gr.at[step], r_gr.at[step], at_r(dx, dy, dc))

    def gram_end(step):
        arrived(gram_r.at[step, 1:16], r_gr.at[step])
        gram = gram_r[step, 0]
        for n in range(1, 2 * NZ):
            gram = gram + gram_r[step, n]
        return inverse_factor(unpack(gram))

    gram_start(0, image)

    def product(dz, chunk):
        rows = pl.ds(pl.multiple_of(lax.rem(z - dz + NQ, NQ) * PAIR, PAIR), PAIR)
        out = jnp.dot(lhs_pair[dz], tiles[chunk, rows, :], preferred_element_type=F32)
        return out[0:K] + out[K : 2 * K]

    def ready(dz):
        first = lax.rem(z - dz + NQ, NQ) * 2
        for dy in range(2):
            if dz or dy:
                arrived(raw_all.at[j_slot(dz, dy)], r_rw.at[dz, dy])
        lhs_pair[dz, :, 0:OWN] = raw_all[first]
        lhs_pair[dz, :, OWN:PAIR] = raw_all[first + 1]

    ready(0)
    for chunk in range(4):
        out_acc[chunk] = product(0, chunk)
    ready(1)
    ready(3)
    for chunk in (3, 2):
        out_acc[chunk] += product(1, chunk) + product(3, chunk)
    gram_middle(0)
    ready(2)
    for chunk in (3, 2):
        to_sibling(1, chunk, out_acc[chunk] + product(2, chunk))
    to_owners(1, 3)
    for chunk in (1, 0):
        to_sibling(1, chunk, out_acc[chunk] + product(1, chunk) + product(3, chunk) + product(2, chunk))
        to_owners(1, chunk + 1)
    to_owners(1, 0)
    inverse = gram_end(0)
    image = gathered(1)
    image = jnp.dot(inverse, image, precision=HIGH, preferred_element_type=F32)
    gram_start(1, image)
    gram_middle(1)
    inverse = gram_end(1)
    vec_ref[...] = jnp.dot(inverse, image, precision=HIGH, preferred_element_type=F32)

    sent(u_i.at[0:15], s_i)
    sent(u_j.at[0:7], s_j)
    sent(start_all.at[0:7], s_st)
    sent(part.at[1:8], s_pt)
    sent(raw_all.at[0:7], s_rw)
    for step in range(2):
        sent(sib_send.at[step], s_sb.at[step])
        sent(sum_send.at[step, 1:8], s_sm.at[step])
        sent(gram_c.at[step, 1:8], s_gc.at[step])
        sent(gram_r.at[step, 1:16], s_gr.at[step])


def local(embeddings, start_vectors):
    dma = pltpu.SemaphoreType.DMA
    vmem = pltpu.VMEM
    vectors, degrees = pl.pallas_call(
        kernel,
        out_shape=(jax.ShapeDtypeStruct((K, OWN), F32), jax.ShapeDtypeStruct((1, OWN), F32)),
        in_specs=[pl.BlockSpec(memory_space=vmem)] * 2,
        out_specs=(pl.BlockSpec(memory_space=vmem), pl.BlockSpec(memory_space=vmem)),
        scratch_shapes=[
            vmem((NQ * NQ, OWN, E), BF16),
            vmem((NZ, OWN, E), BF16),
            vmem((NQ, J, WIDE), BF16),
            vmem((J, 128), F32),
            vmem((NZ, K, OWN), F32),
            vmem((NZ, NZ, OWN), F32),
            vmem((2, NZ, OWN), F32),
            vmem((K, J), BF16),
            vmem((NQ, 2 * K, PAIR), BF16),
            vmem((NQ, K, WIDE), F32),
            vmem((2, NZ, K, OWN), F32),
            vmem((2, NZ, K, OWN), F32),
            vmem((2, NZ, K, OWN), F32),
            vmem((2, NZ, K, OWN), F32),
            vmem((NZ, 2 * K, OWN), BF16),
            vmem((2, NZ, 8, 128), F32),
            vmem((2, 2 * NZ, 8, 128), F32),
            dma, dma((2 * NZ,)),
            dma, dma((NQ, 2)),
            dma, dma,
            dma, dma,
            dma((2,)), dma((2, NQ)),
            dma((2,)), dma((2,)),
            dma, dma((NQ, 2)),
            dma((2,)), dma((2,)),
            dma((2,)), dma((2,)),
        ],
        compiler_params=pltpu.CompilerParams(
            collective_id=0, has_side_effects=True, vmem_limit_bytes=56 * 2**20
        ),
        name="subspace",
    )(embeddings, start_vectors)
    return (vectors, degrees.reshape(OWN))


def solution(mesh):
    return jax.shard_map(
        local,
        mesh=mesh,
        in_specs=(P(("row", "col"), None), P(None, ("row", "col"))),
        out_specs=(P(None, ("row", "col")), P(("row", "col"))),
        check_vma=False,
    )
```

time: 555 us -> 81.1 us (0.15)
  blocking collectives: 232 us -> 0 us
  waiting for transfers between devices: 208 us -> 0 us
  Pallas kernels: 0 us -> 77.6 us
  matrix products: 66.3 us -> 0 us
  other arithmetic: 25.6 us -> 0.6 us
  between operations: 14.5 us -> 0.65 us
    unnamed x6 -> x0, waiting for transfers between devices: 135 us -> none
    psum x2 -> x0, blocking collectives: 132 us -> none  [local(): gram = lax.psum(local_gram, ('row', 'col'))]
    pallas_call x0 -> x1, Pallas kernels: none -> 77.6 us  [local(): pl.pallas_call(kernel, out_shape=(jax.ShapeDtypeStruct((K, OWN), F32), ja...]
    all_gather x2 -> x0, waiting for transfers between devices: 72.9 us -> none  [the longest x1 47.5 us: local(): row_emb = lax.all_gather(own_unit, 'col', axis=0, tiled=True)]
    dot_general x14 -> x0, matrix products: 65.1 us -> none  [the longest x10 39.4 us: one_piece(): lax.dot_general(piece, col_emb, (((1,), (1,)), ((), ())), preferred_eleme...]
    unnamed x1 -> x0, blocking collectives: 58.2 us -> none
    all_gather x2 -> x0, blocking collectives: 41.8 us -> none  [local(): lax.all_gather(scaled, 'row', axis=1, tiled=True)]
    another operation x10 -> x0, other arithmetic: 13.4 us -> none  [the longest x6 7.19 us: local(): lower = jnp.linalg.cholesky(gram)]
  transfers between devices with their start and end apart: 4 -> 0, of which waited for: 4 -> 0; matrix products, arithmetic and copies ran while one was open for 0% -> 0% of each run, Pallas kernels for 0% -> 0%
where the time goes in v3:
time: 81.1 us; the launch traced here: 80.9 us
  Pallas kernels  77.6 us (96%)
  local copies, waits for them, and re-layouts  2.08 us (3%)
    pallas_call x1, Pallas kernels, local(): pl.pallas_call(kernel, out_shape=(jax.ShapeDtypeStruct((K, OWN), F32), ja...  77.6 us
    unnamed x3, local copies, waits for them, and re-layouts  2.08 us

profile of v3, /device:TPU:1, one launch (start us, length us, event | category | flops | bytes accessed | tf_op | source)
XLA Modules:
  0.0 80.9 jit_solution(11115787600431388037)
XLA Ops:
  0.6 77.6 %subspace.1 = (f32[32,320]{1,0:T(8,128)}, f32[1,320]{1,0:T(1,128)}) custom-call(bf16[320,256]{1,0:T(8,128)(2,1)} %emb_ref.1, f32[32,320]{1,0:T(8,128)} %start_ref.1), custom_call_target="tpu_custom_call" | custom-call | tf_op jit(solution)/shard_map/subspace/pallas_call | solution.py:353
  78.3 0.0 copy-start
  78.3 0.7 copy-done
  78.9 0.6 reduce
  79.5 1.4 %copy.5 = f32[32,320]{1,0:T(8,128)} copy(f32[32,320]{1,0:T(8,128)} %get-tuple-element.8) | data formatting | bytes 81920
Async XLA Ops:
  78.3 0.7 copy-start

commit v4 on v3

--- a/solution.py
+++ b/solution.py
@@ -11,7 +11,7 @@
 PLACES = ((0, 0), (0, 1), (1, 0), (3, 0), (2, 0), (1, 1), (3, 1), (2, 1))
 E = 256
 OWN = 320
-HALF = OWN // 2
+PAD = 384
 NZ = 8
 NQ = 4
 J = NZ * OWN
@@ -37,19 +37,36 @@
 
 
 def inverse_factor(gram):
-    rows = lax.broadcasted_iota(jnp.int32, (K, K), 0)
-    columns = lax.broadcasted_iota(jnp.int32, (K, K), 1)
-    eye = (rows == columns).astype(F32)
-    work = jnp.concatenate([gram, eye], axis=1)
-    below = lax.broadcasted_iota(jnp.int32, (K, 1), 0)
-    pivots = jnp.ones((K, 1), F32)
-    for k in range(K):
-        pivot = work[k : k + 1, k : k + 1]
-        column = work[:, k : k + 1]
-        factor = jnp.where(below > k, column / pivot, 0.0)
-        pivots = jnp.where(below == k, pivot, pivots)
-        work = work - factor * work[k : k + 1, :]
-    return work[:, K : 2 * K] * (1.0 / jnp.sqrt(pivots))
+    shape = (8, 2 * K)
+    ranks = lax.broadcasted_iota(jnp.int32, (8, K), 0)
+    lanes = lax.broadcasted_iota(jnp.int32, (8, K), 1)
+    rank = lax.broadcasted_iota(jnp.int32, shape, 0)
+    work = [
+        jnp.concatenate([gram[8 * b : 8 * b + 8], (lanes == ranks + 8 * b).astype(F32)], axis=1) for b in range(4)
+    ]
+    done = []
+    for b in range(4):
+        rows = [jnp.broadcast_to(work[b][i : i + 1], shape) for i in range(8)]
+        columns = [
+            [jnp.broadcast_to(work[c][:, 8 * b + i : 8 * b + i + 1], shape) for c in range(b, 4)] for i in range(8)
+        ]
+        corner = [[jnp.broadcast_to(columns[j][0][i : i + 1], shape) for j in range(i + 1)] for i in range(8)]
+        pivots = corner[0][0]
+        for i in range(8):
+            pivots = jnp.where(rank == i, corner[i][i], pivots)
+            inverse = 1.0 / corner[i][i]
+            factors = [column * inverse for column in columns[i]]
+            factors[0] = jnp.where(rank > i, factors[0], 0.0)
+            for j in range(i + 1, 8):
+                factor = corner[j][i] * inverse
+                rows[j] = rows[j] - factor * rows[i]
+                columns[j] = [old - own * corner[j][i] for old, own in zip(columns[j], factors)]
+                for k in range(i + 1, j + 1):
+                    corner[j][k] = corner[j][k] - factor * corner[k][i]
+            for c in range(b, 4):
+                work[c] = work[c] - factors[c - b] * rows[i]
+        done.append(work[b] * (1.0 / jnp.sqrt(pivots)))
+    return jnp.concatenate(done, axis=0)[:, K : 2 * K]
 
 
 def kernel(
@@ -96,7 +113,7 @@
         ).wait_send()
 
     barrier = pltpu.get_barrier_semaphore()
-    neighbours = [at_r(1, 0), at_r(3, 0), at_r(0, 1), at_c(1, 0), at_c(3, 0), at_c(0, 1), sibling]
+    neighbours = [at_r(*place) for place in PLACES[1:5]] + [at_c(*place) for place in PLACES[1:]] + [sibling]
     for device in neighbours:
         pl.semaphore_signal(barrier, inc=1, device_id=device, device_id_type=MESH)
 
@@ -105,17 +122,16 @@
     unit = (values * lax.rsqrt(power + 1e-06) * (1.0 / math.sqrt(E))).astype(BF16)
     u_i[0] = unit
     u_j[mine] = unit
-    start_all[mine] = start_ref[...]
+    start_all[mine, :, 0:OWN] = start_ref[...]
     acc[...] = jnp.zeros_like(acc)
     pl.semaphore_wait(barrier, len(neighbours))
 
     def i_slot(dx, dy, dc=0):
         return 2 * PLACES.index((dx % NQ, dy)) + dc
 
-    def row_piece(dx, dy, step, flip, half=None):
-        rows = pl.ds(0, OWN) if half is None else pl.ds(half * HALF, HALF)
+    def row_piece(dx, dy, step, flip):
         to = i_slot(dx + step, dy ^ flip)
-        push(u_i.at[i_slot(dx, dy), rows], u_i.at[to, rows], s_i, r_i.at[to], at_r(step, flip))
+        push(u_i.at[i_slot(dx, dy)], u_i.at[to], s_i, r_i.at[to], at_r(step, flip))
 
     def row_over(dx, dy):
         push(u_i.at[i_slot(dx, dy)], u_i.at[i_slot(dx, dy, 1)], s_i, r_i.at[i_slot(dx, dy, 1)], sibling)
@@ -123,97 +139,84 @@
     def row_here(dx, dy, dc=0):
         arrived(u_i.at[i_slot(dx, dy, dc)], r_i.at[i_slot(dx, dy, dc)])
 
-    def col_piece(dz, dy, step, flip, half=None):
-        rows = pl.ds(0, OWN) if half is None else pl.ds(half * HALF, HALF)
+    def col_piece(dz, dy, step, flip):
         slot = j_slot(dz, dy)
-        push(u_j.at[slot, rows], u_j.at[slot, rows], s_j, r_j.at[(dz + step) % NQ, dy ^ flip], at_c(step, flip))
-
-    def col_over(dz, dy):
-        pass
+        push(u_j.at[slot], u_j.at[slot], s_j, r_j.at[(dz + step) % NQ, dy ^ flip], at_c(step, flip))
 
     def col_here(dz, dy):
         arrived(u_j.at[j_slot(dz, dy)], r_j.at[dz, dy])
 
-    def event(here, piece, over, d, dy):
-        here(d, dy)
-        if d in (1, 3) and dy == 0:
-            piece(d, 0, d, 0, 0 if d == 1 else 1)
-            pl.when(core == 1)(lambda: piece(d, 0, 0, 1))
-        elif (d, dy) == (0, 1):
+    def onward(piece, d, dy):
+        if (d, dy) == (0, 1):
 
             @pl.when(core == 0)
             def _():
-                piece(0, 1, 1, 0)
-                piece(0, 1, 3, 0)
-
-        elif (d, dy) == (2, 0):
-            pl.when(core == 1)(lambda: piece(2, 0, 0, 1))
-        elif d in (1, 3):
-            pl.when(core == 0)(lambda: piece(d, 1, d, 0, 0 if d == 1 else 1))
-        over(d, dy)
+                for step in (1, 3, 2):
+                    piece(0, 1, step, 0)
+
+        elif dy == 0:
+            pl.when(core == 1)(lambda: piece(d, 0, 0, 1))
 
     def on_row(dx, dy):
-        event(row_here, row_piece, row_over, dx, dy)
+        row_here(dx, dy)
+        onward(row_piece, dx, dy)
+        row_over(dx, dy)
 
     def on_col(dz, dy):
-        event(col_here, col_piece, col_over, dz, dy)
-
-    def tile(chunk, slot):
+        col_here(dz, dy)
+        onward(col_piece, dz, dy)
+
+    def tile(chunk, slot, low=0, high=WIDE):
         rows_j = pl.ds(pl.multiple_of(slot * OWN, OWN), OWN)
-        block = u_i[pl.ds(NQ * chunk, NQ)].reshape(WIDE, E)
+        block = u_i[NQ * chunk + low // OWN : NQ * chunk + high // OWN].reshape(high - low, E)
         value = jnp.exp2(dot_nt(u_j[slot], block) * RATE)
-        tiles[chunk, rows_j, :] = value.astype(BF16)
+        tiles[chunk, rows_j, low:high] = value.astype(BF16)
         total = acc[rows_j, :]
-        for lane in range(0, WIDE, 128):
+        for lane in range(0, high - low, 128):
             total = total + value[:, lane : lane + 128]
         acc[rows_j, :] = total
 
-    def tile_range(first, last, count, place):
-        def body(n, carry):
-            tile(first + lax.rem(n, last - first), j_slot(*place(n // (last - first))))
-            return carry
-
-        lax.fori_loop(0, count * (last - first), body, 0)
-
-    def near(n):
-        return (n // 2) * (2 * (n % 2) + 1), (1 - n // 2) * (n % 2)
-
-    def beside(n):
-        return 2 * n + 1, 1
+    def tile_range(first, last, places, low=0, high=WIDE):
+        for dz, dy in places:
+            for chunk in range(first, last):
+                tile(chunk, j_slot(dz, dy), low, high)
+
+    near, beside = PLACES[0:4], PLACES[5:7]
 
     row_over(0, 0)
-    for piece in (row_piece, col_piece):
-        piece(0, 0, 0, 1)
-        piece(0, 0, 1, 0)
-        piece(0, 0, 3, 0)
+    for step, flip in ((0, 1), (1, 0), (3, 0), (2, 0)):
+        row_piece(0, 0, step, flip)
+        col_piece(0, 0, step, flip)
     for place in PLACES[1:4]:
         on_row(*place)
         on_col(*place)
-    for dx, dy in PLACES[0:2]:
-        row_here(dx, dy, 1)
-    tile_range(0, 1, 4, near)
-    for dx, dy in PLACES[2:4]:
-        row_here(dx, dy, 1)
+    row_here(0, 0, 1)
+    row_here(0, 1, 1)
+    tile_range(0, 1, near)
+    row_here(1, 0, 1)
+    row_here(3, 0, 1)
+    tile_range(1, 2, near[0:2])
     on_row(2, 0)
     on_col(2, 0)
-    tile_range(1, 2, 4, near)
+    for dz, dy in offsets_c:
+        push(start_all.at[mine], start_all.at[mine], s_st, r_st, at_c(dz, dy))
+    tile_range(1, 2, near[2:4])
+    tile_range(0, 2, PLACES[4:5])
     for place in PLACES[5:7]:
         on_row(*place)
         on_col(*place)
-    tile_range(0, 2, 2, beside)
+    tile_range(0, 2, beside)
     row_here(2, 0, 1)
     row_here(1, 1, 1)
-    tile_range(2, 3, 4, near)
+    tile_range(2, 3, PLACES[0:7])
+    row_here(3, 1, 1)
+    tile_range(3, 4, PLACES[0:7], 0, PAIR)
+    on_row(2, 1)
     on_col(2, 1)
-    for dz, dy in offsets_c:
-        push(start_all.at[mine], start_all.at[mine], s_st, r_st, at_c(dz, dy))
-    on_row(2, 1)
-    tile_range(2, 3, 2, beside)
-    row_here(3, 1, 1)
+    tile_range(0, 3, PLACES[7:8])
+    tile_range(3, 4, PLACES[7:8], 0, PAIR)
     row_here(2, 1, 1)
-    tile_range(3, 4, 4, near)
-    tile_range(3, 4, 2, beside)
-    tile_range(0, 4, 2, lambda n: (2, n))
+    tile_range(3, 4, PLACES, PAIR, WIDE)
     arrived(start_all.at[0:7], r_st)
 
     ones = jnp.ones((8, 128), BF16)
@@ -224,41 +227,41 @@
             top = left.astype(BF16)
             left = left - top.astype(F32)
             total = total + dot_nt(ones, top)
-        part[0, slot : slot + 1, :] = total[0:1, :]
+        part[0, slot : slot + 1, 0:OWN] = total[0:1, :]
     for n, (dz, dy) in enumerate(offsets_c):
         push(part.at[0], part.at[n + 1], s_pt, r_pt, at_c(dz, dy))
     arrived(part.at[1:8], r_pt)
-    degrees = part[0]
+    degrees = part[0, :, 0:OWN]
     for n in range(1, NZ):
-        degrees = degrees + part[n]
+        degrees = degrees + part[n, :, 0:OWN]
     scales = 1.0 / jnp.sqrt(degrees)
     scale_all[0] = scales
     scale_all[1] = degrees * math.exp(-8.0)
     deg_ref[...] = scale_all[1, pl.ds(mine, 1), :]
     scale = scale_all[0, pl.ds(mine, 1), :]
     for slot in range(NZ):
-        lhs[:, slot * OWN : (slot + 1) * OWN] = (start_all[slot] * scales[slot : slot + 1, :]).astype(BF16)
+        lhs[:, slot * OWN : (slot + 1) * OWN] = (start_all[slot, :, 0:OWN] * scales[slot : slot + 1, :]).astype(BF16)
 
     def to_sibling(step, chunk, out):
         pair = pl.ds(2 * chunk, 2)
         for sub in range(2):
-            sum_send[step, 2 * chunk + sub] = out[:, sub * PAIR : sub * PAIR + OWN]
-            sib_send[step, 2 * chunk + sub] = out[:, sub * PAIR + OWN : (sub + 1) * PAIR]
+            sum_send[step, 2 * chunk + sub, :, 0:OWN] = out[:, sub * PAIR : sub * PAIR + OWN]
+            sib_send[step, 2 * chunk + sub, :, 0:OWN] = out[:, sub * PAIR + OWN : (sub + 1) * PAIR]
         push(sib_send.at[step, pair], sib_recv.at[step, pair], s_sb.at[step], r_sb.at[step, chunk], sibling)
 
     def to_owners(step, chunk):
         arrived(sib_recv.at[step, pl.ds(2 * chunk, 2)], r_sb.at[step, chunk])
         for n in (2 * chunk + 1, 2 * chunk):
             dx, dy = PLACES[n]
-            sum_send[step, n] += sib_recv[step, n]
+            sum_send[step, n, :, 0:OWN] += sib_recv[step, n, :, 0:OWN]
             if n:
                 push(sum_send.at[step, n], sum_recv.at[step, n], s_sm.at[step], r_sm.at[step], at_r(-dx, dy))
 
     def gathered(step):
         arrived(sum_recv.at[step, 1:8], r_sm.at[step])
-        total = sum_send[step, 0]
+        total = sum_send[step, 0, :, 0:OWN]
         for n in range(1, NZ):
-            total = total + sum_recv[step, n]
+            total = total + sum_recv[step, n, :, 0:OWN]
         return total * scale
 
     for chunk in (3, 2, 1, 0):
@@ -270,8 +273,8 @@
 
     raw = image * scale
     high = raw.astype(BF16)
-    raw_all[mine, 0:K, :] = high
-    raw_all[mine, K : 2 * K, :] = (raw - high.astype(F32)).astype(BF16)
+    raw_all[mine, 0:K, 0:OWN] = high
+    raw_all[mine, K : 2 * K, 0:OWN] = (raw - high.astype(F32)).astype(BF16)
     for dz, dy in ((0, 1), (1, 1), (3, 1), (2, 1), (2, 0), (1, 0), (3, 0)):
         push(raw_all.at[mine], raw_all.at[mine], s_rw, r_rw.at[dz, dy], at_c(dz, dy))
 
@@ -308,8 +311,8 @@
         for dy in range(2):
             if dz or dy:
                 arrived(raw_all.at[j_slot(dz, dy)], r_rw.at[dz, dy])
-        lhs_pair[dz, :, 0:OWN] = raw_all[first]
-        lhs_pair[dz, :, OWN:PAIR] = raw_all[first + 1]
+        lhs_pair[dz, :, 0:OWN] = raw_all[first, :, 0:OWN]
+        lhs_pair[dz, :, OWN:PAIR] = raw_all[first + 1, :, 0:OWN]
 
     ready(0)
     for chunk in range(4):
@@ -352,7 +355,7 @@
     vmem = pltpu.VMEM
     vectors, degrees = pl.pallas_call(
         kernel,
-        out_shape=(jax.ShapeDtypeStruct((K, OWN), F32), jax.ShapeDtypeStruct((1, OWN), F32)),
+        out_shape=(vmem((K, OWN), F32), vmem((1, OWN), F32)),
         in_specs=[pl.BlockSpec(memory_space=vmem)] * 2,
         out_specs=(pl.BlockSpec(memory_space=vmem), pl.BlockSpec(memory_space=vmem)),
         scratch_shapes=[
@@ -360,17 +363,17 @@
             vmem((NZ, OWN, E), BF16),
             vmem((NQ, J, WIDE), BF16),
             vmem((J, 128), F32),
-            vmem((NZ, K, OWN), F32),
-            vmem((NZ, NZ, OWN), F32),
+            vmem((NZ, K, PAD), F32),
+            vmem((NZ, NZ, PAD), F32),
             vmem((2, NZ, OWN), F32),
             vmem((K, J), BF16),
             vmem((NQ, 2 * K, PAIR), BF16),
             vmem((NQ, K, WIDE), F32),
-            vmem((2, NZ, K, OWN), F32),
-            vmem((2, NZ, K, OWN), F32),
-            vmem((2, NZ, K, OWN), F32),
-            vmem((2, NZ, K, OWN), F32),
-            vmem((NZ, 2 * K, OWN), BF16),
+            vmem((2, NZ, K, PAD), F32),
+            vmem((2, NZ, K, PAD), F32),
+            vmem((2, NZ, K, PAD), F32),
+            vmem((2, NZ, K, PAD), F32),
+            vmem((NZ, 2 * K, PAD), BF16),
             vmem((2, NZ, 8, 128), F32),
             vmem((2, 2 * NZ, 8, 128), F32),
             dma, dma((2 * NZ,)),

time: 81.1 us -> 72.4 us (0.89)
  Pallas kernels: 77.6 us -> 70.4 us
  local copies, waits for them, and re-layouts: 2.08 us -> 0.62 us
    pallas_call x1, Pallas kernels: 77.6 us -> 70.4 us  [local(): pl.pallas_call(kernel, out_shape=(vmem((K, OWN), F32), vmem((1, OWN), F32...]
    unnamed x3 -> x1, local copies, waits for them, and re-layouts: 2.08 us -> 0.62 us
where the time goes in v4:
time: 72.4 us; the launch traced here: 72.2 us
  Pallas kernels  70.4 us (97%)
    pallas_call x1, Pallas kernels, local(): pl.pallas_call(kernel, out_shape=(vmem((K, OWN), F32), vmem((1, OWN), F32...  70.4 us

profile of v4, /device:TPU:1, one launch (start us, length us, event | category | flops | bytes accessed | tf_op | source)
XLA Modules:
  0.0 72.2 jit_solution(15985967239969282115)
XLA Ops:
  0.6 70.4 %subspace.1 = (f32[32,320]{1,0:T(8,128)S(1)}, f32[1,320]{1,0:T(1,128)S(1)}) custom-call(bf16[320,256]{1,0:T(8,128)(2,1)} %emb_ref.1, f32[32,320]{1,0:T(8,128)} %start_ref.1), custom_call_target="tpu_custom_call" | custom-call | tf_op jit(solution)/shard_map/subspace/pallas_call | solution.py:356
  71.0 0.6 copy.5
  71.6 0.6 reduce

commit v5 on v4

--- a/solution.py
+++ b/solution.py
@@ -72,8 +72,8 @@
 def kernel(
     emb_ref, start_ref, vec_ref, deg_ref,
     u_i, u_j, tiles, acc, start_all, part, scale_all, lhs, lhs_pair, out_acc,
-    sib_send, sib_recv, sum_send, sum_recv, raw_all, gram_c, gram_r,
-    s_i, r_i, s_j, r_j, s_st, r_st, s_pt, r_pt, s_sb, r_sb, s_sm, r_sm, s_rw, r_rw, s_gc, r_gc, s_gr, r_gr,
+    send, recv, own_ref, sib_send, sib_recv, sum_send, sum_recv, raw_all, gram_c, gram_r,
+    s_i, r_i, s_j, r_j, s_st, r_st, s_pt, r_pt, s_1, r_1, s_sb, r_sb, s_sm, r_sm, s_rw, r_rw, s_gc, r_gc, s_gr, r_gr,
 ):
     row = lax.axis_index("row")
     col = lax.axis_index("col")
@@ -113,7 +113,7 @@
         ).wait_send()
 
     barrier = pltpu.get_barrier_semaphore()
-    neighbours = [at_r(*place) for place in PLACES[1:5]] + [at_c(*place) for place in PLACES[1:]] + [sibling]
+    neighbours = [at(*place) for at in (at_r, at_c) for place in PLACES[1:5]] + [sibling]
     for device in neighbours:
         pl.semaphore_signal(barrier, inc=1, device_id=device, device_id_type=MESH)
 
@@ -122,7 +122,7 @@
     unit = (values * lax.rsqrt(power + 1e-06) * (1.0 / math.sqrt(E))).astype(BF16)
     u_i[0] = unit
     u_j[mine] = unit
-    start_all[mine, :, 0:OWN] = start_ref[...]
+    start_all[mine, :, 0:OWN] = start_ref[...].astype(BF16)
     acc[...] = jnp.zeros_like(acc)
     pl.semaphore_wait(barrier, len(neighbours))
 
@@ -198,8 +198,6 @@
     tile_range(1, 2, near[0:2])
     on_row(2, 0)
     on_col(2, 0)
-    for dz, dy in offsets_c:
-        push(start_all.at[mine], start_all.at[mine], s_st, r_st, at_c(dz, dy))
     tile_range(1, 2, near[2:4])
     tile_range(0, 2, PLACES[4:5])
     for place in PLACES[5:7]:
@@ -213,11 +211,12 @@
     tile_range(3, 4, PLACES[0:7], 0, PAIR)
     on_row(2, 1)
     on_col(2, 1)
+    for dz, dy in offsets_c:
+        push(start_all.at[mine], start_all.at[mine], s_st, r_st, at_c(dz, dy))
     tile_range(0, 3, PLACES[7:8])
     tile_range(3, 4, PLACES[7:8], 0, PAIR)
     row_here(2, 1, 1)
     tile_range(3, 4, PLACES, PAIR, WIDE)
-    arrived(start_all.at[0:7], r_st)
 
     ones = jnp.ones((8, 128), BF16)
     for slot in range(NZ):
@@ -239,37 +238,26 @@
     scale_all[1] = degrees * math.exp(-8.0)
     deg_ref[...] = scale_all[1, pl.ds(mine, 1), :]
     scale = scale_all[0, pl.ds(mine, 1), :]
+    arrived(start_all.at[0:7], r_st)
     for slot in range(NZ):
-        lhs[:, slot * OWN : (slot + 1) * OWN] = (start_all[slot, :, 0:OWN] * scales[slot : slot + 1, :]).astype(BF16)
-
-    def to_sibling(step, chunk, out):
-        pair = pl.ds(2 * chunk, 2)
-        for sub in range(2):
-            sum_send[step, 2 * chunk + sub, :, 0:OWN] = out[:, sub * PAIR : sub * PAIR + OWN]
-            sib_send[step, 2 * chunk + sub, :, 0:OWN] = out[:, sub * PAIR + OWN : (sub + 1) * PAIR]
-        push(sib_send.at[step, pair], sib_recv.at[step, pair], s_sb.at[step], r_sb.at[step, chunk], sibling)
-
-    def to_owners(step, chunk):
-        arrived(sib_recv.at[step, pl.ds(2 * chunk, 2)], r_sb.at[step, chunk])
-        for n in (2 * chunk + 1, 2 * chunk):
-            dx, dy = PLACES[n]
-            sum_send[step, n, :, 0:OWN] += sib_recv[step, n, :, 0:OWN]
-            if n:
-                push(sum_send.at[step, n], sum_recv.at[step, n], s_sm.at[step], r_sm.at[step], at_r(-dx, dy))
-
-    def gathered(step):
-        arrived(sum_recv.at[step, 1:8], r_sm.at[step])
-        total = sum_send[step, 0, :, 0:OWN]
-        for n in range(1, NZ):
-            total = total + sum_recv[step, n, :, 0:OWN]
-        return total * scale
+        lhs[:, slot * OWN : (slot + 1) * OWN] = (start_all[slot, :, 0:OWN].astype(F32) * scales[slot : slot + 1, :]).astype(BF16)
 
     for chunk in (3, 2, 1, 0):
-        to_sibling(0, chunk, jnp.dot(lhs[...], tiles[chunk], preferred_element_type=F32))
-        if chunk < 3:
-            to_owners(0, chunk + 1)
-    to_owners(0, 0)
-    image = gathered(0)
+        out = jnp.dot(lhs[...], tiles[chunk], preferred_element_type=F32)
+        for sub in range(NQ):
+            slot = NQ * chunk + sub
+            block = out[:, sub * OWN : (sub + 1) * OWN]
+            if slot == 0:
+                own_ref[...] = block
+            else:
+                dx, dy = PLACES[slot // 2]
+                send[slot, :, 0:OWN] = block.astype(BF16)
+                push(send.at[slot], recv.at[slot], s_1, r_1, at_r(-dx, dy, slot % 2))
+    arrived(recv.at[1:16], r_1)
+    image = own_ref[...]
+    for slot in range(1, 2 * NZ):
+        image = image + recv[slot, :, 0:OWN].astype(F32)
+    image = image * scale
 
     raw = image * scale
     high = raw.astype(BF16)
@@ -301,6 +289,21 @@
 
     gram_start(0, image)
 
+    def to_sibling(chunk, out):
+        pair = pl.ds(2 * chunk, 2)
+        for sub in range(2):
+            sum_send[2 * chunk + sub, :, 0:OWN] = out[:, sub * PAIR : sub * PAIR + OWN]
+            sib_send[2 * chunk + sub, :, 0:OWN] = out[:, sub * PAIR + OWN : (sub + 1) * PAIR]
+        push(sib_send.at[pair], sib_recv.at[pair], s_sb, r_sb.at[chunk], sibling)
+
+    def to_owners(chunk):
+        arrived(sib_recv.at[pl.ds(2 * chunk, 2)], r_sb.at[chunk])
+        for n in (2 * chunk + 1, 2 * chunk):
+            dx, dy = PLACES[n]
+            sum_send[n, :, 0:OWN] += sib_recv[n, :, 0:OWN]
+            if n:
+                push(sum_send.at[n], sum_recv.at[n], s_sm, r_sm, at_r(-dx, dy))
+
     def product(dz, chunk):
         rows = pl.ds(pl.multiple_of(lax.rem(z - dz + NQ, NQ) * PAIR, PAIR), PAIR)
         out = jnp.dot(lhs_pair[dz], tiles[chunk, rows, :], preferred_element_type=F32)
@@ -319,19 +322,21 @@
         out_acc[chunk] = product(0, chunk)
     ready(1)
     ready(3)
-    for chunk in (3, 2):
+    for chunk in range(4):
         out_acc[chunk] += product(1, chunk) + product(3, chunk)
     gram_middle(0)
     ready(2)
-    for chunk in (3, 2):
-        to_sibling(1, chunk, out_acc[chunk] + product(2, chunk))
-    to_owners(1, 3)
-    for chunk in (1, 0):
-        to_sibling(1, chunk, out_acc[chunk] + product(1, chunk) + product(3, chunk) + product(2, chunk))
-        to_owners(1, chunk + 1)
-    to_owners(1, 0)
+    for chunk in (3, 2, 1, 0):
+        to_sibling(chunk, out_acc[chunk] + product(2, chunk))
+        if chunk < 3:
+            to_owners(chunk + 1)
+    to_owners(0)
     inverse = gram_end(0)
-    image = gathered(1)
+    arrived(sum_recv.at[1:8], r_sm)
+    image = sum_send[0, :, 0:OWN]
+    for n in range(1, NZ):
+        image = image + sum_recv[n, :, 0:OWN]
+    image = image * scale
     image = jnp.dot(inverse, image, precision=HIGH, preferred_element_type=F32)
     gram_start(1, image)
     gram_middle(1)
@@ -343,9 +348,10 @@
     sent(start_all.at[0:7], s_st)
     sent(part.at[1:8], s_pt)
     sent(raw_all.at[0:7], s_rw)
+    sent(send.at[1:16], s_1)
+    sent(sib_send, s_sb)
+    sent(sum_send.at[1:8], s_sm)
     for step in range(2):
-        sent(sib_send.at[step], s_sb.at[step])
-        sent(sum_send.at[step, 1:8], s_sm.at[step])
         sent(gram_c.at[step, 1:8], s_gc.at[step])
         sent(gram_r.at[step, 1:16], s_gr.at[step])
 
@@ -363,16 +369,19 @@
             vmem((NZ, OWN, E), BF16),
             vmem((NQ, J, WIDE), BF16),
             vmem((J, 128), F32),
-            vmem((NZ, K, PAD), F32),
+            vmem((NZ, K, PAD), BF16),
             vmem((NZ, NZ, PAD), F32),
             vmem((2, NZ, OWN), F32),
             vmem((K, J), BF16),
             vmem((NQ, 2 * K, PAIR), BF16),
             vmem((NQ, K, WIDE), F32),
-            vmem((2, NZ, K, PAD), F32),
-            vmem((2, NZ, K, PAD), F32),
-            vmem((2, NZ, K, PAD), F32),
-            vmem((2, NZ, K, PAD), F32),
+            vmem((2 * NZ, K, PAD), BF16),
+            vmem((2 * NZ, K, PAD), BF16),
+            vmem((K, OWN), F32),
+            vmem((NZ, K, PAD), F32),
+            vmem((NZ, K, PAD), F32),
+            vmem((NZ, K, PAD), F32),
+            vmem((NZ, K, PAD), F32),
             vmem((NZ, 2 * K, PAD), BF16),
             vmem((2, NZ, 8, 128), F32),
             vmem((2, 2 * NZ, 8, 128), F32),
@@ -380,8 +389,9 @@
             dma, dma((NQ, 2)),
             dma, dma,
             dma, dma,
-            dma((2,)), dma((2, NQ)),
-            dma((2,)), dma((2,)),
+            dma, dma,
+            dma, dma((NQ,)),
+            dma, dma,
             dma, dma((NQ, 2)),
             dma((2,)), dma((2,)),
             dma((2,)), dma((2,)),

time: 72.4 us -> 71.6 us (0.989)
  Pallas kernels: 70.4 us -> 69.6 us
    pallas_call x1, Pallas kernels: 70.4 us -> 69.6 us  [local(): pl.pallas_call(kernel, out_shape=(vmem((K, OWN), F32), vmem((1, OWN), F32...]
where the time goes in v5:
time: 71.6 us; the launch traced here: 71.5 us
  Pallas kernels  69.6 us (97%)
    pallas_call x1, Pallas kernels, local(): pl.pallas_call(kernel, out_shape=(vmem((K, OWN), F32), vmem((1, OWN), F32...  69.6 us

profile of v5, /device:TPU:1, one launch (start us, length us, event | category | flops | bytes accessed | tf_op | source)
XLA Modules:
  0.0 71.5 jit_solution(10626615214483739561)
XLA Ops:
  0.6 69.6 %subspace.1 = (f32[32,320]{1,0:T(8,128)S(1)}, f32[1,320]{1,0:T(1,128)S(1)}) custom-call(bf16[320,256]{1,0:T(8,128)(2,1)} %emb_ref.1, f32[32,320]{1,0:T(8,128)} %start_ref.1), custom_call_target="tpu_custom_call" | custom-call | tf_op jit(solution)/shard_map/subspace/pallas_call | solution.py:362
  70.2 0.6 copy.5
  70.9 0.6 reduce

commit v6 on v5

--- a/solution.py
+++ b/solution.py
@@ -34,6 +34,18 @@
 
 def unpack(packed):
     return jnp.concatenate([packed[:, K * b : K * b + K] for b in range(4)], axis=0)
+
+
+def fold(wide):
+    n = wide.shape[0]
+    rest = [wide[n // 4 * b : n // 4 * (b + 1), 256:OWN] for b in range(4)]
+    return jnp.concatenate([wide[:, 0:256], jnp.concatenate(rest, axis=1)], axis=0)
+
+
+def unfold(folded):
+    n = folded.shape[0] // 5 * 4
+    rest = [folded[n:, 64 * b : 64 * (b + 1)] for b in range(4)]
+    return jnp.concatenate([folded[0:n], jnp.concatenate(rest, axis=0)], axis=1)
 
 
 def inverse_factor(gram):
@@ -261,8 +273,7 @@
 
     raw = image * scale
     high = raw.astype(BF16)
-    raw_all[mine, 0:K, 0:OWN] = high
-    raw_all[mine, K : 2 * K, 0:OWN] = (raw - high.astype(F32)).astype(BF16)
+    raw_all[mine] = fold(jnp.concatenate([high, (raw - high.astype(F32)).astype(BF16)], axis=0))
     for dz, dy in ((0, 1), (1, 1), (3, 1), (2, 1), (2, 0), (1, 0), (3, 0)):
         push(raw_all.at[mine], raw_all.at[mine], s_rw, r_rw.at[dz, dy], at_c(dz, dy))
 
@@ -292,15 +303,15 @@
     def to_sibling(chunk, out):
         pair = pl.ds(2 * chunk, 2)
         for sub in range(2):
-            sum_send[2 * chunk + sub, :, 0:OWN] = out[:, sub * PAIR : sub * PAIR + OWN]
-            sib_send[2 * chunk + sub, :, 0:OWN] = out[:, sub * PAIR + OWN : (sub + 1) * PAIR]
+            sum_send[2 * chunk + sub] = fold(out[:, sub * PAIR : sub * PAIR + OWN])
+            sib_send[2 * chunk + sub] = fold(out[:, sub * PAIR + OWN : (sub + 1) * PAIR])
         push(sib_send.at[pair], sib_recv.at[pair], s_sb, r_sb.at[chunk], sibling)
 
     def to_owners(chunk):
         arrived(sib_recv.at[pl.ds(2 * chunk, 2)], r_sb.at[chunk])
         for n in (2 * chunk + 1, 2 * chunk):
             dx, dy = PLACES[n]
-            sum_send[n, :, 0:OWN] += sib_recv[n, :, 0:OWN]
+            sum_send[n] += sib_recv[n]
             if n:
                 push(sum_send.at[n], sum_recv.at[n], s_sm, r_sm, at_r(-dx, dy))
 
@@ -314,8 +325,8 @@
         for dy in range(2):
             if dz or dy:
                 arrived(raw_all.at[j_slot(dz, dy)], r_rw.at[dz, dy])
-        lhs_pair[dz, :, 0:OWN] = raw_all[first, :, 0:OWN]
-        lhs_pair[dz, :, OWN:PAIR] = raw_all[first + 1, :, 0:OWN]
+        lhs_pair[dz, :, 0:OWN] = unfold(raw_all[first])
+        lhs_pair[dz, :, OWN:PAIR] = unfold(raw_all[first + 1])
 
     ready(0)
     for chunk in range(4):
@@ -333,10 +344,10 @@
     to_owners(0)
     inverse = gram_end(0)
     arrived(sum_recv.at[1:8], r_sm)
-    image = sum_send[0, :, 0:OWN]
+    total = sum_send[0]
     for n in range(1, NZ):
-        image = image + sum_recv[n, :, 0:OWN]
-    image = image * scale
+        total = total + sum_recv[n]
+    image = unfold(total) * scale
     image = jnp.dot(inverse, image, precision=HIGH, preferred_element_type=F32)
     gram_start(1, image)
     gram_middle(1)
@@ -378,11 +389,11 @@
             vmem((2 * NZ, K, PAD), BF16),
             vmem((2 * NZ, K, PAD), BF16),
             vmem((K, OWN), F32),
-            vmem((NZ, K, PAD), F32),
-            vmem((NZ, K, PAD), F32),
-            vmem((NZ, K, PAD), F32),
-            vmem((NZ, K, PAD), F32),
-            vmem((NZ, 2 * K, PAD), BF16),
+            vmem((NZ, K + K // 4, 256), F32),
+            vmem((NZ, K + K // 4, 256), F32),
+            vmem((NZ, K + K // 4, 256), F32),
+            vmem((NZ, K + K // 4, 256), F32),
+            vmem((NZ, 2 * K + K // 2, 256), BF16),
             vmem((2, NZ, 8, 128), F32),
             vmem((2, 2 * NZ, 8, 128), F32),
             dma, dma((2 * NZ,)),

time: 71.6 us -> 70.6 us (0.986)
  Pallas kernels: 69.6 us -> 68.7 us
    pallas_call x1, Pallas kernels: 69.6 us -> 68.7 us  [local(): pl.pallas_call(kernel, out_shape=(vmem((K, OWN), F32), vmem((1, OWN), F32...]
where the time goes in v6:
time: 70.6 us; the launch traced here: 70.5 us
  Pallas kernels  68.7 us (97%)
    pallas_call x1, Pallas kernels, local(): pl.pallas_call(kernel, out_shape=(vmem((K, OWN), F32), vmem((1, OWN), F32...  68.7 us

profile of v6, /device:TPU:1, one launch (start us, length us, event | category | flops | bytes accessed | tf_op | source)
XLA Modules:
  0.0 70.5 jit_solution(5281795044156432029)
XLA Ops:
  0.6 68.7 %subspace.1 = (f32[32,320]{1,0:T(8,128)S(1)}, f32[1,320]{1,0:T(1,128)S(1)}) custom-call(bf16[320,256]{1,0:T(8,128)(2,1)} %emb_ref.1, f32[32,320]{1,0:T(8,128)} %start_ref.1), custom_call_target="tpu_custom_call" | custom-call | tf_op jit(solution)/shard_map/subspace/pallas_call | solution.py:373
  69.3 0.6 copy.5
  69.9 0.6 reduce

commit v7 on v6

--- a/solution.py
+++ b/solution.py
@@ -234,7 +234,7 @@
     for slot in range(NZ):
         left = acc[slot * OWN : (slot + 1) * OWN, :]
         total = jnp.zeros((8, OWN), F32)
-        for _ in range(3):
+        for _ in range(2):
             top = left.astype(BF16)
             left = left - top.astype(F32)
             total = total + dot_nt(ones, top)
@@ -274,7 +274,7 @@
     raw = image * scale
     high = raw.astype(BF16)
     raw_all[mine] = fold(jnp.concatenate([high, (raw - high.astype(F32)).astype(BF16)], axis=0))
-    for dz, dy in ((0, 1), (1, 1), (3, 1), (2, 1), (2, 0), (1, 0), (3, 0)):
+    for dz, dy in ((0, 1), (1, 0), (3, 0), (1, 1), (3, 1), (2, 0), (2, 1)):
         push(raw_all.at[mine], raw_all.at[mine], s_rw, r_rw.at[dz, dy], at_c(dz, dy))
 
     def gram_start(step, image):

time: 70.6 us -> 69.9 us (0.990)
  no operation moved by 1% of the time
where the time goes in v7:
time: 69.9 us; the launch traced here: 69.8 us
  Pallas kernels  68 us (97%)
    pallas_call x1, Pallas kernels, local(): pl.pallas_call(kernel, out_shape=(vmem((K, OWN), F32), vmem((1, OWN), F32...  68 us

profile of v7, /device:TPU:1, one launch (start us, length us, event | category | flops | bytes accessed | tf_op | source)
XLA Modules:
  0.0 69.8 jit_solution(8700342598885899151)
XLA Ops:
  0.6 68.0 %subspace.1 = (f32[32,320]{1,0:T(8,128)S(1)}, f32[1,320]{1,0:T(1,128)S(1)}) custom-call(bf16[320,256]{1,0:T(8,128)(2,1)} %emb_ref.1, f32[32,320]{1,0:T(8,128)} %start_ref.1), custom_call_target="tpu_custom_call" | custom-call | tf_op jit(solution)/shard_map/subspace/pallas_call | solution.py:373
  68.6 0.6 copy.5
  69.2 0.6 reduce
